TPU v7x, 128 devices: a whole 4x4x4 slice. The times are simulated.
128 devices in a mesh: dp: 8 (over z, core), tensor: 16 (over x, y).
Axes of the slice: x: 4, y: 4, z: 4, core: 2. Of those that a mesh axis runs over, the one named last changes fastest.
Arguments:
- activations: float32 [512, 32, 16384], P('dp', None, 'tensor'), may hold values from -6 to 6
- gradients: float32 [512, 32, 16384], P('dp', None, 'tensor'), may hold values from -6 to 6
- proj_in: float32 [16384, 128], P('tensor'), may hold values from -0.046875 to 0.046875
- proj_out: float32 [16384, 128], P('tensor'), may hold values from -0.046875 to 0.046875
- damping: float32 [16384], P(('dp', 'tensor')), may hold values from 1 to 100
- queries: float32 [16384, 512], P(('dp', 'tensor')), may hold values from -6 to 6
Outputs:
- solution: float32 [16384, 512], P(('dp', 'tensor'))
- residual: float32 [16384, 512], P(('dp', 'tensor'))
- gram: float32 [16384, 8, 2048], P('dp', None, 'tensor')
All inputs are finite; a program needn't handle non-finite values. Where the computation divides by a largest or mean magnitude, that divisor is 1e-20 or more.
Results may differ from a plain program's by a relative error of at most 0.00013.
Values sent between devices are 32-bit elements; how exact they have to be, the bound alone decides.
A program may use at most 128 MiB of HBM per device.

v0:
```python
import jax
import jax.numpy as jnp
from jax import lax
from jax.sharding import PartitionSpec as P

ITERS = 2


HIGHEST = lax.Precision.HIGHEST


def shards(activations, gradients, proj_in, proj_out, damping, queries):
    seq_local, tok_len, width_shard = activations.shape
    proj_rank = proj_in.shape[1]
    act_rows = activations.reshape(seq_local * tok_len, width_shard)
    grad_rows = gradients.reshape(seq_local * tok_len, gradients.shape[2])
    proj_acts = jnp.dot(act_rows, proj_in, precision=HIGHEST, preferred_element_type=jnp.float32)
    proj_grads = jnp.dot(grad_rows, proj_out, precision=HIGHEST, preferred_element_type=jnp.float32)
    summed = lax.psum_scatter(
        jnp.stack((proj_grads, proj_acts), axis=1), "tensor", scatter_dimension=0, tiled=True
    )
    own_seqs = summed.shape[0] // tok_len
    summed = summed.reshape(own_seqs, tok_len, 2, proj_rank)
    features = jnp.einsum("sti,stj->sij", summed[:, :, 0], summed[:, :, 1], precision=HIGHEST)
    features = features.reshape(own_seqs, proj_rank * proj_rank)
    feature_slab = lax.all_to_all(
        features, ("dp", "tensor"), split_axis=1, concat_axis=0, tiled=True
    )
    seq_count = feature_slab.shape[0]
    slab_width = feature_slab.shape[1]
    grid_rows = lax.all_gather(feature_slab, "tensor", axis=1, tiled=True)
    gram_tile = (
        jnp.einsum(
            "sr,sc->rc",
            grid_rows,
            lax.all_gather(feature_slab, "dp", axis=1, tiled=True),
            precision=HIGHEST,
        )
        / seq_count
    )
    row_totals = (
        lax.psum_scatter(
            jnp.sum(jnp.abs(gram_tile), axis=1), "tensor", scatter_dimension=0, tiled=True
        )
        + damping
    )
    bound_low = lax.pmin(jnp.min(damping), ("dp", "tensor"))
    bound_high = lax.pmax(jnp.max(row_totals), ("dp", "tensor"))
    ratio_low = bound_low / bound_high
    center_value = (1.0 + ratio_low) / 2.0
    half_width = (1.0 - ratio_low) / 2.0
    spread_ratio = center_value / half_width
    ratio_now = 1.0 / spread_ratio
    solution = jnp.zeros_like(queries)
    residual = queries
    direction = queries / center_value
    for iteration in range(ITERS):
        solution = solution + direction
        grid_direction = lax.all_gather(direction, "dp", axis=0, tiled=True)
        gram_part = lax.psum_scatter(
            jnp.dot(gram_tile, grid_direction, precision=HIGHEST),
            "tensor",
            scatter_dimension=0,
            tiled=True,
        )
        applied = gram_part + damping[:, None] * direction
        residual = residual - applied / bound_high
        if iteration + 1 < ITERS:
            ratio_next = 1.0 / (2.0 * spread_ratio - ratio_now)
            direction = (
                ratio_next * ratio_now * direction + 2.0 * ratio_next / half_width * residual
            )
            ratio_now = ratio_next
    column_blocks = gram_tile.shape[1] // slab_width
    gram_out = gram_tile.reshape(gram_tile.shape[0], column_blocks, slab_width)
    return (solution, residual, gram_out)


def solution(mesh):
    return jax.shard_map(
        shards,
        mesh=mesh,
        in_specs=(
            P("dp", None, "tensor"),
            P("dp", None, "tensor"),
            P("tensor", None),
            P("tensor", None),
            P(("dp", "tensor")),
            P(("dp", "tensor"), None),
        ),
        out_specs=(P(("dp", "tensor"), None), P(("dp", "tensor"), None), P("dp", None, "tensor")),
        check_vma=False,
    )
```

profile of v0, /device:TPU:0, one launch (start us, length us, event | category | flops | bytes accessed | tf_op | source)
XLA Modules:
  0.0 644.6 jit_solution(12345942717165749688)
XLA Ops:
  7.2 1.0 copy-done
  8.2 9.2 %convolution_bitcast_fusion = f32[2048,1,128]{2,0,1:T(8,128)S(1)} fusion(f32[2048,1024]{1,0:T(8,128)} %bitcast.29, f32[1024,128]{1,0:T(8,128)S(1)} %copy-done), kind=kOutput, calls=%fused_computation.2 | convolution fusion | flops 3221225472 | bytes 9961472 | tf_op jit(solution)/shard_map/dot_general | solution.py:17
  17.5 7.0 %convolution_bitcast_fusion.1 = f32[2048,1,128]{2,0,1:T(8,128)S(1)} fusion(f32[2048,1024]{1,0:T(8,128)S(1)} %bitcast.30, f32[1024,128]{1,0:T(8,128)S(1)} %copy-done.4), kind=kOutput, calls=%fused_computation.3 | convolution fusion | flops 3221225472 | bytes 9961472 | tf_op jit(solution)/shard_map/dot_general | solution.py:18
  24.5 1.5 pad_maximum_fusion
  26.0 76.8 %reduce-scatter.4.cloned.1.call-done = f32[128,2,128]{2,0,1:T(8,128)} async-done(((f32[2048,2,128]{2,0,1:T(8,128)}), f32[128,2,128]{2,0,1:T(8,128)}) %reduce-scatter.4.cloned.1.call-update) | async-done | bytes 131088 | tf_op jit(solution)/shard_map/reduce_scatter | solution.py:19
  102.8 1.5 fusion
  104.4 18.8 %all_to_all.16 = f32[4,128,128]{2,0,1:T(4,128)} all-to-all(f32[4,128,128]{2,0,1:T(4,128)S(1)} %copy.12), channel_id=1, replica_groups=mesh['dp'=8,'tensor'=16] {'dp','tensor'}, dimensions={1} | all-to-all | bytes 524288 | tf_op jit(solution)/shard_map/all_to_all | solution.py:26
  123.3 0.7 all-gather.5.cloned.1.call-update
  125.3 21.5 %all-gather.7.cloned.1.call-done = f32[512,1024]{1,0:T(8,128)} async-done(((f32[512,128]{1,0:T(8,128)}), f32[512,1024]{1,0:T(8,128)}) %all-gather.7.cloned.1.call-update) | async-done | bytes 2097168 | tf_op jit(solution)/shard_map/all_gather | solution.py:36
  146.7 60.6 %all-gather.5.cloned.1.call-done = f32[512,2048]{1,0:T(8,128)} async-done(((f32[512,128]{1,0:T(8,128)}), f32[512,2048]{1,0:T(8,128)}) %all-gather.5.cloned.1.call-update) | async-done | bytes 4194320 | tf_op jit(solution)/shard_map/all_gather | solution.py:31
  207.4 18.2 %abs_reduce_fusion = (f32[2048]{0:T(1024)S(1)}, f32[2048,1024]{0,1:T(8,128)}) fusion(f32[512,2048]{1,0:T(8,128)} %all-gather.5.cloned.1.call-done, f32[512,1024]{1,0:T(8,128)} %all-gather.7.cloned.1.call-done), kind=kOutput, calls=%fused_computation | convolution fusion | flops 12891191296 | bytes 14688256 | tf_op jit(solution)/shard_map/sr,sc->rc/dot_general | solution.py:33
  225.6 38.6 %all-reduce = f32[2048]{0:T(1024)S(1)} all-reduce(f32[2048]{0:T(1024)S(1)} %get-tuple-element.16), channel_id=3, replica_groups=mesh['dp'=8,'tensor'=16] {'tensor'}, use_global_device_ids=true, to_apply=%region_4.0.clone | all-reduce | flops 2048 | bytes 16384
  264.9 62.7 %pmin.7 = f32[]{:T(128)} all-reduce(f32[]{:T(128)} %get-tuple-element.13), channel_id=1, replica_groups=mesh['dp'=8,'tensor'=16] {'dp','tensor'}, use_global_device_ids=true, to_apply=%region_1.0 | all-reduce | flops 1 | bytes 8 | tf_op jit(solution)/shard_map/pmin | solution.py:47
  327.6 64.7 %pmax.7 = f32[]{:T(128)} all-reduce(f32[]{:T(128)} %get-tuple-element.12), channel_id=1, replica_groups=mesh['dp'=8,'tensor'=16] {'dp','tensor'}, use_global_device_ids=true, to_apply=%region_6.0 | all-reduce | flops 1 | bytes 8 | tf_op jit(solution)/shard_map/pmax | solution.py:48
  393.7 0.7 broadcast_divide_fusion
  394.7 21.3 %all-gather.9.cloned.1.call-done = f32[1024,512]{1,0:T(8,128)} async-done(((f32[128,512]{1,0:T(8,128)}), f32[1024,512]{1,0:T(8,128)}) %all-gather.9.cloned.1.call-update) | async-done | bytes 2097168 | tf_op jit(solution)/shard_map/all_gather | solution.py:59
  416.0 17.6 %fusion.3 = f32[2048,512]{1,0:T(8,128)} fusion(f32[2048,1024]{0,1:T(8,128)} %get-tuple-element.17, f32[1024,512]{1,0:T(8,128)} %all-gather.9.cloned.1.call-done), kind=kOutput, calls=%fused_computation.15 | convolution fusion | flops 12884901888 | bytes 14680064 | tf_op jit(solution)/shard_map/dot_general | solution.py:61
  433.8 77.8 %reduce-scatter.6.cloned.1.call-done = f32[128,512]{1,0:T(8,128)} async-done(((f32[2048,512]{1,0:T(8,128)}), f32[128,512]{1,0:T(8,128)}) %reduce-scatter.6.cloned.1.call-update) | async-done | bytes 262160 | tf_op jit(solution)/shard_map/reduce_scatter | solution.py:60
  511.7 2.5 multiply_add_fusion
  514.5 24.6 %all-gather.11.cloned.1.call-done = f32[1024,512]{1,0:T(8,128)} async-done(((f32[128,512]{1,0:T(8,128)}), f32[1024,512]{1,0:T(8,128)}) %all-gather.11.cloned.1.call-update) | async-done | bytes 2097168 | tf_op jit(solution)/shard_map/all_gather | solution.py:59
  539.0 17.6 %fusion.4 = f32[2048,512]{1,0:T(8,128)} fusion(f32[2048,1024]{0,1:T(8,128)} %get-tuple-element.17, f32[1024,512]{1,0:T(8,128)} %all-gather.11.cloned.1.call-done), kind=kOutput, calls=%fused_computation.16 | convolution fusion | flops 12884901888 | bytes 14680064 | tf_op jit(solution)/shard_map/dot_general | solution.py:61
  556.7 9.3 %copy.13 = f32[2048,8,128]{2,1,0:T(8,128)} copy(f32[2048,8,128]{0,2,1:T(8,128)} %bitcast.28) | data formatting | bytes 16777216
  566.0 68.7 %reduce-scatter.8.cloned.1.call-done = f32[128,512]{1,0:T(8,128)} async-done(((f32[2048,512]{1,0:T(8,128)}), f32[128,512]{1,0:T(8,128)}) %reduce-scatter.8.cloned.1.call-update) | async-done | bytes 262160 | tf_op jit(solution)/shard_map/reduce_scatter | solution.py:60
  634.7 2.6 divide_subtract_fusion
  (29 shorter events, 2.3 us)
Async XLA Ops:
  7.2 1.0 copy-start
  7.2 95.6 %reduce-scatter.4.cloned.1.call-start = ((), (), s32[]{:S(2)}) async-start(), calls=%async_computation.4 | async-start | bytes 2228224 | tf_op jit(solution)/shard_map/reduce_scatter | solution.py:19
  8.2 9.2 %copy-start.1 = (f32[64,32,1024]{2,1,0:T(8,128)S(1)}, f32[64,32,1024]{2,1,0:T(8,128)}, u32[]{:S(2)}) copy-start(f32[64,32,1024]{2,1,0:T(8,128)} %param.7) | copy-start | bytes 25165828
  8.2 9.2 %copy-start.4 = (f32[1024,128]{1,0:T(8,128)S(1)}, f32[1024,128]{1,0:T(8,128)}, u32[]{:S(2)}) copy-start(f32[1024,128]{1,0:T(8,128)} %param.9) | copy-start | bytes 1572868
  24.5 99.6 %copy-start.6 = (u32[128]{0:T(128)S(1)}, u32[128]{0:T(128)}, u32[]{:S(2)}) copy-start(u32[128]{0:T(128)} %constant.18) | copy-start | bytes 1540
  25.9 120.8 %all-gather.7.cloned.1.call-start = ((), (), s32[]{:S(2)}) async-start(), calls=%async_computation.6 | async-start | bytes 2359296 | tf_op jit(solution)/shard_map/all_gather | solution.py:36
  123.2 84.1 %all-gather.5.cloned.1.call-start = ((), (), s32[]{:S(2)}) async-start(), calls=%async_computation.5 | async-start | bytes 4456448 | tf_op jit(solution)/shard_map/all_gather | solution.py:31
  124.0 292.0 %all-gather.9.cloned.1.call-start = ((), (), s32[]{:S(2)}) async-start(), calls=%async_computation.7 | async-start | bytes 2359296 | tf_op jit(solution)/shard_map/all_gather | solution.py:59
  125.3 138.9 %copy-start.5 = (f32[128]{0:T(128)S(1)}, f32[128]{0:T(128)}, u32[]{:S(2)}) copy-start(f32[128]{0:T(128)} %param.10) | copy-start | bytes 1540
  125.3 268.4 %copy-start.2 = (f32[128,512]{1,0:T(8,128)S(1)}, f32[128,512]{1,0:T(8,128)}, u32[]{:S(2)}) copy-start(f32[128,512]{1,0:T(8,128)} %param.11) | copy-start | bytes 786436
  394.5 117.2 %reduce-scatter.6.cloned.1.call-start = ((), (), s32[]{:S(2)}) async-start(), calls=%async_computation.8 | async-start | bytes 4456448 | tf_op jit(solution)/shard_map/reduce_scatter | solution.py:60
  433.6 105.4 %all-gather.11.cloned.1.call-start = ((), (), s32[]{:S(2)}) async-start(), calls=%async_computation.9 | async-start | bytes 2359296 | tf_op jit(solution)/shard_map/all_gather | solution.py:59
  514.2 120.5 %reduce-scatter.8.cloned.1.call-start = ((), (), s32[]{:S(2)}) async-start(), calls=%async_computation.10 | async-start | bytes 4456448 | tf_op jit(solution)/shard_map/reduce_scatter | solution.py:60
  556.7 78.1 %copy-start.3 = (f32[128,512]{1,0:T(8,128)S(1)}, f32[128,512]{1,0:T(8,128)}, u32[]{:S(2)}) copy-start(f32[128,512]{1,0:T(8,128)} %reduce-scatter.6.cloned.1.call-done) | copy-start | bytes 786436
Sparse Core Ops, SparseCore 0:
  26.1 76.6 reduce-scatter.3
  123.3 23.3 all-gather.6
  149.1 58.2 all-gather.4
  394.6 21.3 all-gather.8
  433.7 77.8 reduce-scatter.5
  514.3 24.6 all-gather.10
  556.8 77.8 reduce-scatter.7
where the time goes:
time: 653 us; the launch traced here: 645 us
  waiting for transfers between devices  352 us (54%)
  blocking collectives  185 us (28%)
  matrix products  71 us (11%)
  between operations  16.9 us (3%)
  local copies, waits for them, and re-layouts  11.1 us (2%)
  other arithmetic  7.94 us (1%)
    reduce_scatter x2, waiting for transfers between devices, shards(): lax.psum_scatter(jnp.dot(gram_tile, grid_direction, precision=HIGHEST), '...  147 us
    reduce_scatter x1, waiting for transfers between devices, shards(): lax.psum_scatter(jnp.stack((proj_grads, proj_acts), axis=1), 'tensor', sc...  76.8 us
    pmax x1, blocking collectives, shards(): bound_high = lax.pmax(jnp.max(row_totals), ('dp', 'tensor'))  64.7 us
    pmin x1, blocking collectives, shards(): bound_low = lax.pmin(jnp.min(damping), ('dp', 'tensor'))  62.7 us
    all_gather x1, waiting for transfers between devices, shards(): grid_rows = lax.all_gather(feature_slab, 'tensor', axis=1, tiled=True)  60.6 us
    all_gather x2, waiting for transfers between devices, shards(): grid_direction = lax.all_gather(direction, 'dp', axis=0, tiled=True)  45.8 us
    unnamed x1, blocking collectives  38.6 us
    dot_general x2, matrix products, shards(): jnp.dot(gram_tile, grid_direction, precision=HIGHEST)  35.2 us
  transfers between devices with their start and end apart: 7, of which 7 were waited for; matrix products, arithmetic and copies ran while one was open for 2% of the time, Pallas kernels for 0%

commit v1 on v0

v1 whole, which is shorter than its diff:
```python
import jax
import jax.numpy as jnp
from jax import lax
from jax.experimental import pallas as pl
from jax.experimental.pallas import tpu as pltpu
from jax.sharding import PartitionSpec as P

MESH = pl.DeviceIdType.MESH
F32 = jnp.float32
BF16 = jnp.bfloat16
ORDER = (1, 3, 2)
NT = (((1,), (1,)), ((), ()))
NN = (((1,), (0,)), ((), ()))
TN = (((0,), (0,)), ((), ()))


def vmem():
    return pl.BlockSpec(memory_space=pltpu.VMEM)


def hbm():
    return pl.BlockSpec(memory_space=pl.ANY)


def params(collective_id, mib):
    return pltpu.CompilerParams(
        collective_id=collective_id, has_side_effects=True, vmem_limit_bytes=mib * 2**20
    )


def place():
    d, t = lax.axis_index("dp"), lax.axis_index("tensor")
    return d, t, lax.div(d, 2), lax.rem(d, 2), lax.div(t, 4), lax.rem(t, 4)


def shift(value, by, size):
    return lax.rem(value + by, size)


def greet(peers):
    barrier = pltpu.get_barrier_semaphore()
    for peer in peers:
        pl.semaphore_signal(barrier, inc=1, device_id=peer, device_id_type=MESH)


def greeted(count):
    pl.semaphore_wait(pltpu.get_barrier_semaphore(), count)


def send(src, dst, send_sem, recv_sem, peer):
    copy = pltpu.make_async_remote_copy(
        src_ref=src,
        dst_ref=dst,
        send_sem=send_sem,
        recv_sem=recv_sem,
        device_id=peer,
        device_id_type=MESH,
    )
    copy.start()
    return copy


def parts(value):
    high = value.astype(BF16)
    low = (value - high.astype(F32)).astype(BF16)
    return high, low


def mm(a, b, dims):
    return lax.dot_general(a, b, dims, preferred_element_type=F32)


def few_rows(value, weight_high, weight_low, dims):
    rows = value.shape[0]
    high, low = parts(value)
    both = mm(jnp.concatenate((high, low), axis=0), weight_high, dims)
    return both[:rows] + both[rows:] + mm(high, weight_low, dims)


def project_kernel(
    act, grad, pin, pout, q, damp, fd, qr,
    gbuf, abuf, wg, wa, yg, ya, r1g, r1a, s2g, s2a, r2g, r2a, qs, fsend, frecv,
    in_sem, s1_sem, r1_sem, s2_sem, r2_sem, sq_sem, rq_sem, sf_sem, rf_sem,
):
    d, t, z, c, x, y = place()
    loads = []
    for n, o in enumerate(ORDER + (0,)):
        g = pltpu.make_async_copy(grad.at[shift(x, o, 4)], gbuf.at[n], in_sem.at[0, n])
        a = pltpu.make_async_copy(act.at[:, shift(y, o, 4)], abuf.at[n], in_sem.at[1, n])
        g.start()
        a.start()
        loads.append((g, a))
    peers = [(d, shift(t, o, 16)) for o in range(1, 16)]
    greet(peers)
    row = lax.broadcasted_iota(jnp.int32, (128, 128), 0)
    column = lax.broadcasted_iota(jnp.int32, (128, 128), 1)
    order = (row == 16 * lax.rem(column, 8) + lax.div(column, 8)).astype(BF16)
    high, low = parts(pout[...])
    wg[:, :128] = mm(high, order, NN).astype(BF16)
    wg[:, 128:] = mm(low, order, NN).astype(BF16)
    high, low = parts(pin[...])
    wa[:, :128] = high
    wa[:, 128:] = low
    for n in range(16):
        qs[n, :32] = q[:, pl.ds(128 * (n // 4), 128)].T[32 * (n % 4) : 32 * (n % 4) + 32]
        qs[n, 32:] = jnp.broadcast_to(damp[...], (8, 128))
    greeted(15)
    copies = []
    for n in range(15):
        to = shift(t, n + 1, 16)
        copies.append(send(qs.at[to], qr.at[t], sq_sem.at[n], rq_sem.at[n], (d, to)))
    qr[t] = qs[t]

    def project(buf, weight, out, n):
        def step(m, carry):
            high, low = parts(buf[n, m])
            first = mm(high, weight[...], NN)
            second = mm(low, weight[:, :128], NN)
            out[n, m] = first[:, :128] + first[:, 128:] + second
            return carry

        lax.fori_loop(0, 4, step, 0)

    firsts = []
    for n, o in enumerate(ORDER + (0,)):
        loads[n][0].wait()
        project(gbuf, wg, yg, n)
        if o:
            firsts.append(
                send(yg.at[n], r1g.at[n], s1_sem.at[0, n], r1_sem.at[0, n], (d, shift(x, o, 4) * 4 + y))
            )
        loads[n][1].wait()
        project(abuf, wa, ya, n)
        if o:
            firsts.append(
                send(ya.at[n], r1a.at[n], s1_sem.at[1, n], r1_sem.at[1, n], (d, x * 4 + shift(y, o, 4)))
            )
    for copy in firsts:
        copy.wait()

    def total(own, got, at):
        return own[3, at] + got[0, at] + (got[1, at] + got[2, at])

    seconds = []
    for n, o in enumerate(ORDER):
        yy, xx = shift(y, o, 4), shift(x, o, 4)
        s2g[n] = total(yg, r1g, yy)
        seconds.append(send(s2g.at[n], r2g.at[n], s2_sem.at[0, n], r2_sem.at[0, n], (d, x * 4 + yy)))
        s2a[n] = total(ya, r1a, xx)
        seconds.append(send(s2a.at[n], r2a.at[n], s2_sem.at[1, n], r2_sem.at[1, n], (d, xx * 4 + y)))
    pg = total(yg, r1g, y)
    pa = total(ya, r1a, x)
    for copy in seconds:
        copy.wait()
    pg = pg + r2g[0] + (r2g[1] + r2g[2])
    pa = pa + r2a[0] + (r2a[1] + r2a[2])
    for s in range(4):
        gh, gl = parts(pg[32 * s : 32 * s + 32].T)
        ah, al = parts(pa[32 * s : 32 * s + 32])
        feature = mm(gh, ah, NN) + mm(gh, al, NN) + mm(gl, ah, NN)
        fsend[:, s] = feature.reshape(16, 8, 128)
    for n in range(15):
        to = shift(t, n + 1, 16)
        copies.append(send(fsend.at[to], frecv.at[t], sf_sem.at[n], rf_sem.at[n], (d, to)))
    frecv[t] = fsend[t]
    for copy in copies:
        copy.wait()
    for k in range(8):
        fd[k] = frecv[:, :, k, :].reshape(64, 128)


def project(act, grad, pin, pout, q, damp):
    sem = pltpu.SemaphoreType.DMA
    return pl.pallas_call(
        project_kernel,
        out_shape=(
            jax.ShapeDtypeStruct((8, 64, 128), F32),
            jax.ShapeDtypeStruct((16, 40, 128), F32),
        ),
        in_specs=[hbm(), hbm(), vmem(), vmem(), vmem(), vmem()],
        out_specs=(vmem(), vmem()),
        scratch_shapes=[
            pltpu.VMEM((4, 4, 128, 1024), F32),
            pltpu.VMEM((4, 4, 128, 1024), F32),
            pltpu.VMEM((1024, 256), BF16),
            pltpu.VMEM((1024, 256), BF16),
            pltpu.VMEM((4, 4, 128, 128), F32),
            pltpu.VMEM((4, 4, 128, 128), F32),
            pltpu.VMEM((3, 4, 128, 128), F32),
            pltpu.VMEM((3, 4, 128, 128), F32),
            pltpu.VMEM((3, 128, 128), F32),
            pltpu.VMEM((3, 128, 128), F32),
            pltpu.VMEM((3, 128, 128), F32),
            pltpu.VMEM((3, 128, 128), F32),
            pltpu.VMEM((16, 40, 128), F32),
            pltpu.VMEM((16, 4, 8, 128), F32),
            pltpu.VMEM((16, 4, 8, 128), F32),
            sem((2, 4)),
            sem((2, 3)),
            sem((2, 3)),
            sem((2, 3)),
            sem((2, 3)),
            sem((15,)),
            sem((15,)),
            sem((15,)),
            sem((15,)),
        ],
        compiler_params=params(1, 56),
    )(act, grad, pin, pout, q, damp)


def gather_kernel(fd, rows, cols, slab, s1, r1, sc, rc, sx, rx, s3, r3):
    d, t, z, c, x, y = place()
    dp_peers = [(shift(d, o, 8), t) for o in range(1, 8)]
    xs = [(d, shift(x, o, 4) * 4 + y) for o in ORDER]
    ys = [(d, x * 4 + shift(y, o, 4)) for o in ORDER]
    greet(dp_peers + xs + ys)
    greeted(13)
    firsts = []
    for n in range(7):
        to = shift(d, n + 1, 8)
        firsts.append(send(fd.at[to], slab.at[d], s1.at[n], r1.at[n], (to, t)))
    slab[d] = fd[d]
    cols[d] = fd[...]
    zs = [send(fd, cols.at[d], sc.at[n], rc.at[n], (shift(z, o, 4) * 2 + c, t)) for n, o in enumerate(ORDER)]
    other = (z * 2 + 1 - c, t)
    cores = [send(fd, cols.at[d], sx.at[3], rx.at[3], other)]
    for copy in firsts:
        copy.wait()
    for n in range(4):
        piece = slab[2 * n : 2 * n + 2].reshape(128, 128).T
        rows[t, 0, :, 128 * n : 128 * n + 128] = piece[:64]
        rows[t, 1, :, 128 * n : 128 * n + 128] = piece[64:]

    def hop(half, at, first, second, peer):
        return send(
            rows.at[at, half], rows.at[at, half], s3.at[half, first, second], r3.at[half, first, second], peer
        )

    firsts, rest = {}, []
    for n in range(3):
        firsts[0, n] = hop(0, t, n, 3, xs[n])
        firsts[1, n] = hop(1, t, n, 3, ys[n])
    for n in range(3):
        rest.append(hop(0, t, 3, n, ys[n]))
        rest.append(hop(1, t, 3, n, xs[n]))
    for n, o in enumerate(ORDER):
        firsts[0, n].wait()
        for m in range(3):
            rest.append(hop(0, shift(x, 4 - o, 4) * 4 + y, n, m, ys[m]))
        firsts[1, n].wait()
        for m in range(3):
            rest.append(hop(1, x * 4 + shift(y, 4 - o, 4), n, m, xs[m]))
    for n, o in enumerate(ORDER):
        zs[n].wait()
        from_d = shift(z, 4 - o, 4) * 2 + c
        cores.append(send(cols.at[from_d], cols.at[from_d], sx.at[n], rx.at[n], other))
    for copy in cores + rest:
        copy.wait()


def gather(fd):
    sem = pltpu.SemaphoreType.DMA
    return pl.pallas_call(
        gather_kernel,
        out_shape=(
            jax.ShapeDtypeStruct((16, 2, 64, 512), F32),
            jax.ShapeDtypeStruct((8, 8, 64, 128), F32),
        ),
        in_specs=[vmem()],
        out_specs=(vmem(), vmem()),
        scratch_shapes=[
            pltpu.VMEM((8, 64, 128), F32),
            sem((7,)),
            sem((7,)),
            sem((3,)),
            sem((3,)),
            sem((4,)),
            sem((4,)),
            sem((2, 4, 4)),
            sem((2, 4, 4)),
        ],
        compiler_params=params(2, 40),
    )(fd)


def gram_kernel(rows, cols, qr, gram, sums, fq, rows_high, rows_low, ch, cl):
    step = pl.program_id(0)

    @pl.when(step == 0)
    def _():
        def fill(n, carry):
            at = pl.ds(pl.multiple_of(n * 64, 64), 64)
            for k in range(8):
                high, low = parts(cols[n, k] * (1.0 / 512))
                ch[at, 128 * k : 128 * k + 128] = high
                cl[at, 128 * k : 128 * k + 128] = low
            return carry

        lax.fori_loop(0, 8, fill, 0)
        fq[...] = jnp.zeros_like(fq)

    high, low = parts(rows[...])
    rows_high[...] = high
    rows_low[...] = low
    total = jnp.zeros((256, 128), F32)
    for k in range(4):
        at = pl.ds(256 * k, 256)
        tile = mm(high, ch[:, at], NN) + mm(high, cl[:, at], NN) + mm(low, ch[:, at], NN)
        gram[:, 2 * k, :] = tile[:, :128]
        gram[:, 2 * k + 1, :] = tile[:, 128:]
        total = total + jnp.abs(tile[:, :128]) + jnp.abs(tile[:, 128:])
    sums[0, 0] = jnp.sum(total[:128].T, axis=0)
    sums[0, 1] = jnp.sum(total[128:].T, axis=0)
    query = jnp.concatenate((qr[0, :32], qr[1, :32]), axis=1)
    fq[...] += few_rows(query, high, low, NN)


def gram_tile(rows, cols, qr):
    return pl.pallas_call(
        gram_kernel,
        grid=(8,),
        out_shape=(
            jax.ShapeDtypeStruct((2048, 8, 128), F32),
            jax.ShapeDtypeStruct((8, 2, 128), F32),
            jax.ShapeDtypeStruct((32, 512), F32),
            jax.ShapeDtypeStruct((2048, 512), BF16),
            jax.ShapeDtypeStruct((2048, 512), BF16),
        ),
        in_specs=[
            pl.BlockSpec((256, 512), lambda n: (n, 0)),
            pl.BlockSpec((8, 8, 64, 128), lambda n: (0, 0, 0, 0)),
            pl.BlockSpec((2, 40, 128), lambda n: (n, 0, 0)),
        ],
        out_specs=(
            pl.BlockSpec((256, 8, 128), lambda n: (n, 0, 0)),
            pl.BlockSpec((1, 2, 128), lambda n: (n, 0, 0)),
            pl.BlockSpec((32, 512), lambda n: (0, 0)),
            pl.BlockSpec((256, 512), lambda n: (n, 0)),
            pl.BlockSpec((256, 512), lambda n: (n, 0)),
        ),
        scratch_shapes=[pltpu.VMEM((512, 1024), BF16), pltpu.VMEM((512, 1024), BF16)],
        compiler_params=pltpu.CompilerParams(vmem_limit_bytes=40 * 2**20),
    )(rows, cols, qr)


def solve_kernel(
    rows_high, rows_low, fq, sums, qr, sol, res,
    fp, got1, got2, sums_all, pt, mine, bounds, out, back,
    s_fq, r_fq, s_fp, r_fp, s_sum, r_sum, s_bound, r_bound, s_out, r_out,
):
    d, t, z, c, x, y = place()
    dp_peers = [(shift(d, o, 8), t) for o in range(1, 8)]
    tensor_peers = [(d, shift(t, o, 16)) for o in range(1, 16)]
    greet(dp_peers + tensor_peers)
    greeted(22)
    copies = [send(fq, got1.at[n], s_fq.at[n], r_fq.at[n], peer) for n, peer in enumerate(dp_peers)]
    sum_copies = [
        send(sums, sums_all.at[n], s_sum.at[n], r_sum.at[n], peer) for n, peer in enumerate(tensor_peers)
    ]
    for copy in copies:
        copy.wait()
    fq_all = fq[...]
    for n in range(7):
        fq_all = fq_all + got1[n]
    fp[...] = jnp.zeros_like(fp)

    def forward(n, carry):
        at = pl.ds(pl.multiple_of(n * 256, 256), 256)
        product = few_rows(fq_all, rows_high[at], rows_low[at], NT) * (1.0 / 512)
        for h in range(2):
            pt[2 * n + h] = product[:, 128 * h : 128 * h + 128] + qr[2 * n + h, 32:33] * qr[2 * n + h, :32]
        value = jnp.concatenate((pt[2 * n], pt[2 * n + 1]), axis=1)
        fp[...] += few_rows(value, rows_high[at], rows_low[at], NN)
        return carry

    lax.fori_loop(0, 8, forward, 0)
    copies = [send(fp, got2.at[n], s_fp.at[n], r_fp.at[n], peer) for n, peer in enumerate(dp_peers)]
    for copy in sum_copies:
        copy.wait()
    row_sums = sums[...]
    for n in range(15):
        row_sums = row_sums + sums_all[n]
    damping = qr[:, 32:33].reshape(16, 128)
    high = jnp.max(row_sums.reshape(16, 128) + damping, axis=(0, 1), keepdims=True)
    low = jnp.min(damping, axis=(0, 1), keepdims=True)
    mine[:8] = jnp.broadcast_to(high, (8, 128))
    mine[8:] = jnp.broadcast_to(low, (8, 128))
    bound_copies = [
        send(mine, bounds.at[n], s_bound.at[n], r_bound.at[n], peer) for n, peer in enumerate(dp_peers)
    ]
    for copy in bound_copies:
        copy.wait()
    bound_high, bound_low = mine[:1], mine[8:9]
    for n in range(7):
        bound_high = jnp.maximum(bound_high, bounds[n, :1])
        bound_low = jnp.minimum(bound_low, bounds[n, 8:9])
    ratio_low = bound_low / bound_high
    center = (1.0 + ratio_low) / 2.0
    half = (1.0 - ratio_low) / 2.0
    spread = center / half
    ratio = 1.0 / spread
    ratio_next = 1.0 / (2.0 * spread - ratio)
    keep = ratio_next * ratio
    add = 2.0 * ratio_next / half
    for copy in copies:
        copy.wait()
    fp_all = fp[...]
    for n in range(7):
        fp_all = fp_all + got2[n]
    fp_all = fp_all / jnp.concatenate([bound_high] * 4, axis=1)

    def finish(n, carry):
        at = pl.ds(pl.multiple_of(n * 256, 256), 256)
        product = few_rows(fp_all, rows_high[at], rows_low[at], NT) * (1.0 / 512)
        for h in range(2):
            query, damp = qr[2 * n + h, :32], qr[2 * n + h, 32:33]
            scaled = pt[2 * n + h] / bound_high
            used = scaled / center
            first = query / center
            residual = query - used
            second = keep * first + add * residual
            out[2 * n + h, 0] = first + second
            applied = (product[:, 128 * h : 128 * h + 128] / center + damp * used) / bound_high
            out[2 * n + h, 1] = residual - (keep * used + add * (scaled - applied))
        return carry

    lax.fori_loop(0, 8, finish, 0)
    copies = []
    for n in range(15):
        to = shift(t, n + 1, 16)
        copies.append(send(out.at[to], back.at[t], s_out.at[n], r_out.at[n], (d, to)))
    back[t] = out[t]
    for copy in copies:
        copy.wait()
    for n in range(4):
        sol[:, 128 * n : 128 * n + 128] = back[4 * n : 4 * n + 4, 0].reshape(128, 128).T
        res[:, 128 * n : 128 * n + 128] = back[4 * n : 4 * n + 4, 1].reshape(128, 128).T


def solve(rows_high, rows_low, fq, sums, qr):
    sem = pltpu.SemaphoreType.DMA
    return pl.pallas_call(
        solve_kernel,
        out_shape=(jax.ShapeDtypeStruct((128, 512), F32), jax.ShapeDtypeStruct((128, 512), F32)),
        in_specs=[vmem()] * 5,
        out_specs=(vmem(), vmem()),
        scratch_shapes=[
            pltpu.VMEM((32, 512), F32),
            pltpu.VMEM((7, 32, 512), F32),
            pltpu.VMEM((7, 32, 512), F32),
            pltpu.VMEM((15, 16, 128), F32),
            pltpu.VMEM((16, 32, 128), F32),
            pltpu.VMEM((16, 128), F32),
            pltpu.VMEM((7, 16, 128), F32),
            pltpu.VMEM((16, 2, 32, 128), F32),
            pltpu.VMEM((16, 2, 32, 128), F32),
            sem((7,)),
            sem((7,)),
            sem((7,)),
            sem((7,)),
            sem((15,)),
            sem((15,)),
            sem((7,)),
            sem((7,)),
            sem((15,)),
            sem((15,)),
        ],
        compiler_params=params(3, 40),
    )(rows_high, rows_low, fq, sums, qr)


def shards(activations, gradients, proj_in, proj_out, damping, queries):
    act = activations.reshape(4, 4, 128, 1024)
    grad = gradients.reshape(4, 4, 128, 1024)
    fd, qr = project(act, grad, proj_in, proj_out, queries, damping.reshape(1, 128))
    rows, cols = gather(fd)
    gram, sums, fq, rows_high, rows_low = gram_tile(rows.reshape(2048, 512), cols, qr)
    answer, residual = solve(rows_high, rows_low, fq, sums.reshape(16, 128), qr)
    return answer, residual, gram


def solution(mesh):
    return jax.shard_map(
        shards,
        mesh=mesh,
        in_specs=(
            P("dp", None, "tensor"),
            P("dp", None, "tensor"),
            P("tensor", None),
            P("tensor", None),
            P(("dp", "tensor")),
            P(("dp", "tensor"), None),
        ),
        out_specs=(P(("dp", "tensor"), None), P(("dp", "tensor"), None), P("dp", None, "tensor")),
        check_vma=False,
    )
```

time: 653 us -> 135 us (0.21); the launches traced: 645 us -> 134 us
  waiting for transfers between devices: 352 us -> 0 us
  blocking collectives: 185 us -> 0 us
  Pallas kernels: 0 us -> 130 us
  matrix products: 71 us -> 0 us
  between operations: 16.9 us -> 0.67 us
  other arithmetic: 7.94 us -> 0 us
  local copies, waits for them, and re-layouts: 11.1 us -> 3.32 us
    reduce_scatter x3 -> x0, waiting for transfers between devices: 223 us -> none  [the longest x2 147 us: shards(): lax.psum_scatter(jnp.dot(gram_tile, grid_direction, precision=HIGHEST), '...]
    pallas_call x0 -> x4, Pallas kernels: none -> 130 us  [the longest x1 42.3 us: gather(): pl.pallas_call(gather_kernel, out_shape=(jax.ShapeDtypeStruct((16, 2, 64,...]
    all_gather x4 -> x0, waiting for transfers between devices: 128 us -> none  [the longest x1 60.6 us: shards(): grid_rows = lax.all_gather(feature_slab, 'tensor', axis=1, tiled=True)]
    dot_general x6 -> x0, matrix products: 71 us -> none  [the longest x2 35.2 us: shards(): jnp.dot(gram_tile, grid_direction, precision=HIGHEST)]
    pmax x1 -> x0, blocking collectives: 64.7 us -> none  [shards(): bound_high = lax.pmax(jnp.max(row_totals), ('dp', 'tensor'))]
    pmin x1 -> x0, blocking collectives: 62.7 us -> none  [shards(): bound_low = lax.pmin(jnp.min(damping), ('dp', 'tensor'))]
    unnamed x1 -> x0, blocking collectives: 38.6 us -> none
    all_to_all x1 -> x0, blocking collectives: 18.8 us -> none  [shards(): lax.all_to_all(features, ('dp', 'tensor'), split_axis=1, concat_axis=0, t...]
  transfers between devices with their start and end apart: 7 -> 0, of which waited for: 7 -> 0; matrix products, arithmetic and copies ran while one was open for 2% -> 0% of each run, Pallas kernels for 0% -> 0%
where the time goes in v1:
time: 135 us; the launch traced here: 134 us
  Pallas kernels  130 us (96%)
  local copies, waits for them, and re-layouts  3.32 us (2%)
    pallas_call x1, Pallas kernels, gather(): pl.pallas_call(gather_kernel, out_shape=(jax.ShapeDtypeStruct((16, 2, 64,...  42.3 us
    pallas_call x1, Pallas kernels, project(): pl.pallas_call(project_kernel, out_shape=(jax.ShapeDtypeStruct((8, 64, 12...  37.7 us
    pallas_call x1, Pallas kernels, solve(): pl.pallas_call(solve_kernel, out_shape=(jax.ShapeDtypeStruct((128, 512),...  36 us
    pallas_call x1, Pallas kernels, gram_tile(): pl.pallas_call(gram_kernel, grid=(8,), out_shape=(jax.ShapeDtypeStruct((2...  14.6 us
    unnamed x6, local copies, waits for them, and re-layouts  3.32 us

profile of v1, /device:TPU:0, one launch (start us, length us, event | category | flops | bytes accessed | tf_op | source)
XLA Modules:
  0.0 134.4 jit_solution(461774287827698257)
XLA Ops:
  0.6 37.7 %shard_map.85 = (f32[8,64,128]{2,1,0:T(8,128)}, f32[16,40,128]{2,1,0:T(8,128)}) custom-call(f32[4,4,128,1024]{3,2,1,0:T(8,128)} %bitcast.7, f32[4,4,128,1024]{3,2,1,0:T(8,128)} %bitcast.8, f32[1024,128]{1,0:T(8,128)} %pin.1, f32[1024,128]{1,0:T(8,128)} %pout.1, f32[128,512]{1,0:T(8,128)} %q.1, f32[1,128]{1,0:T(1,128)} %bitcast.9), custom_call_target="tpu_custom_call" | custom-call | tf_op jit(solution)/shard_map/pallas_call | solution.py:174
  38.3 0.0 copy-start.1
  38.3 0.9 copy-done.1
  39.3 42.3 %shard_map.86 = (f32[16,2,64,512]{3,2,1,0:T(8,128)S(1)}, f32[8,8,64,128]{3,2,1,0:T(8,128)S(1)}) custom-call(f32[8,64,128]{2,1,0:T(8,128)S(1)} %copy-done.1), custom_call_target="tpu_custom_call" | custom-call | tf_op jit(solution)/shard_map/pallas_call | solution.py:264
  81.5 0.0 copy-start
  81.5 1.0 copy-done
  82.5 14.6 %shard_map.87 = (f32[2048,8,128]{2,1,0:T(8,128)}, f32[8,2,128]{2,1,0:T(2,128)S(1)}, f32[32,512]{1,0:T(8,128)S(1)}, bf16[2048,512]{1,0:T(8,128)(2,1)S(1)}, bf16[2048,512]{1,0:T(8,128)(2,1)S(1)}) custom-call(f32[2048,512]{1,0:T(8,128)S(1)} %bitcast.5, f32[8,8,64,128]{3,2,1,0:T(8,128)S(1)} %get-tuple-element.16.cols, f32[16,40,128]{2,1,0:T(8,128)S(1)} %copy-done), custom_call_target="tpu_custom_call" | custom-call | tf_op jit(solution)/shard_map/pallas_call | solution.py:320
  97.1 36.0 %shard_map.88 = (f32[128,512]{1,0:T(8,128)S(1)}, f32[128,512]{1,0:T(8,128)S(1)}) custom-call(bf16[2048,512]{1,0:T(8,128)(2,1)S(1)} %get-tuple-element.18.rows_high, bf16[2048,512]{1,0:T(8,128)(2,1)S(1)} %get-tuple-element.19.rows_low, f32[32,512]{1,0:T(8,128)S(1)} %get-tuple-element.20.fq, f32[16,128]{1,0:T(8,128)S(1)} %bitcast.6, f32[16,40,128]{2,1,0:T(8,128)S(1)} %copy-done), custom_call_target="tpu_custom_call" | custom-call | tf_op jit(solution)/shard_map/pallas_call | solution.py:443
  133.0 0.7 copy.11
  133.7 0.7 copy.12
Async XLA Ops:
  38.3 1.0 copy-start.1
  81.5 1.0 copy-start

commit v2 on v1

v2 whole, which is shorter than its diff:
```python
import jax
import jax.numpy as jnp
from jax import lax
from jax.experimental import pallas as pl
from jax.experimental.pallas import tpu as pltpu
from jax.sharding import PartitionSpec as P

MESH = pl.DeviceIdType.MESH
F32 = jnp.float32
BF16 = jnp.bfloat16
ORDER = (1, 3, 2)
NT = (((1,), (1,)), ((), ()))
NN = (((1,), (0,)), ((), ()))
TN = (((0,), (0,)), ((), ()))


def vmem():
    return pl.BlockSpec(memory_space=pltpu.VMEM)


def hbm():
    return pl.BlockSpec(memory_space=pl.ANY)


def params(collective_id, mib):
    return pltpu.CompilerParams(
        collective_id=collective_id, has_side_effects=True, vmem_limit_bytes=mib * 2**20
    )


def place():
    d, t = lax.axis_index("dp"), lax.axis_index("tensor")
    return d, t, lax.div(d, 2), lax.rem(d, 2), lax.div(t, 4), lax.rem(t, 4)


def shift(value, by, size):
    return lax.rem(value + by, size)


def greet(peers):
    barrier = pltpu.get_barrier_semaphore()
    for peer in peers:
        pl.semaphore_signal(barrier, inc=1, device_id=peer, device_id_type=MESH)


def greeted(count):
    pl.semaphore_wait(pltpu.get_barrier_semaphore(), count)


def send(src, dst, send_sem, recv_sem, peer):
    copy = pltpu.make_async_remote_copy(
        src_ref=src,
        dst_ref=dst,
        send_sem=send_sem,
        recv_sem=recv_sem,
        device_id=peer,
        device_id_type=MESH,
    )
    copy.start()
    return copy


def parts(value):
    high = value.astype(BF16)
    low = (value - high.astype(F32)).astype(BF16)
    return high, low


def mm(a, b, dims):
    return lax.dot_general(a, b, dims, preferred_element_type=F32)


def few_rows(value, weight_high, weight_low, dims):
    rows = value.shape[0]
    high, low = parts(value)
    both = mm(jnp.concatenate((high, low), axis=0), weight_high, dims)
    return both[:rows] + both[rows:] + mm(high, weight_low, dims)


def project_kernel(
    act, grad, pin, pout, q, damp, fd, qr,
    gbuf, abuf, wg, wa, yg, ya, r1g, r1a, s2g, s2a, r2g, r2a, qs, fsend, frecv,
    in_sem, s1_sem, r1_sem, s2_sem, r2_sem, sq_sem, rq_sem, sf_sem, rf_sem,
):
    d, t, z, c, x, y = place()
    loads = []
    for n, o in enumerate(ORDER + (0,)):
        g = pltpu.make_async_copy(grad.at[shift(x, o, 4)], gbuf.at[n], in_sem.at[0, n])
        a = pltpu.make_async_copy(act.at[:, shift(y, o, 4)], abuf.at[n], in_sem.at[1, n])
        g.start()
        a.start()
        loads.append((g, a))
    peers = [(d, shift(t, o, 16)) for o in range(1, 16)]
    greet(peers)
    row = lax.broadcasted_iota(jnp.int32, (128, 128), 0)
    column = lax.broadcasted_iota(jnp.int32, (128, 128), 1)
    order = (row == 16 * lax.rem(column, 8) + lax.div(column, 8)).astype(BF16)
    high, low = parts(pout[...])
    wg[:, :128] = mm(high, order, NN).astype(BF16)
    wg[:, 128:] = mm(low, order, NN).astype(BF16)
    high, low = parts(pin[...])
    wa[:, :128] = high
    wa[:, 128:] = low
    for n in range(16):
        qs[n, :32] = q[:, pl.ds(128 * (n // 4), 128)].T[32 * (n % 4) : 32 * (n % 4) + 32]
        qs[n, 32:] = jnp.broadcast_to(damp[...], (8, 128))
    greeted(15)
    copies = []
    for n in range(15):
        to = shift(t, n + 1, 16)
        copies.append(send(qs.at[to], qr.at[t], sq_sem.at[n], rq_sem.at[n], (d, to)))
    qr[t] = qs[t]

    def project(buf, weight, out, n):
        def step(m, carry):
            high, low = parts(buf[n, m])
            first = mm(high, weight[...], NN)
            second = mm(low, weight[:, :128], NN)
            out[n, m] = first[:, :128] + first[:, 128:] + second
            return carry

        lax.fori_loop(0, 4, step, 0)

    firsts = []
    for n, o in enumerate(ORDER + (0,)):
        loads[n][0].wait()
        project(gbuf, wg, yg, n)
        if o:
            firsts.append(
                send(yg.at[n], r1g.at[n], s1_sem.at[0, n], r1_sem.at[0, n], (d, shift(x, o, 4) * 4 + y))
            )
        loads[n][1].wait()
        project(abuf, wa, ya, n)
        if o:
            firsts.append(
                send(ya.at[n], r1a.at[n], s1_sem.at[1, n], r1_sem.at[1, n], (d, x * 4 + shift(y, o, 4)))
            )
    for copy in firsts:
        copy.wait()

    def total(own, got, at):
        return own[3, at] + got[0, at] + (got[1, at] + got[2, at])

    seconds = []
    for n, o in enumerate(ORDER):
        yy, xx = shift(y, o, 4), shift(x, o, 4)
        s2g[n] = total(yg, r1g, yy)
        seconds.append(send(s2g.at[n], r2g.at[n], s2_sem.at[0, n], r2_sem.at[0, n], (d, x * 4 + yy)))
        s2a[n] = total(ya, r1a, xx)
        seconds.append(send(s2a.at[n], r2a.at[n], s2_sem.at[1, n], r2_sem.at[1, n], (d, xx * 4 + y)))
    pg = total(yg, r1g, y)
    pa = total(ya, r1a, x)
    for copy in seconds:
        copy.wait()
    pg = pg + r2g[0] + (r2g[1] + r2g[2])
    pa = pa + r2a[0] + (r2a[1] + r2a[2])
    for s in range(4):
        gh, gl = parts(pg[32 * s : 32 * s + 32].T)
        ah, al = parts(pa[32 * s : 32 * s + 32])
        feature = mm(gh, ah, NN) + mm(gh, al, NN) + mm(gl, ah, NN)
        fsend[:, s] = feature.reshape(16, 8, 128)
    for n in range(15):
        to = shift(t, n + 1, 16)
        copies.append(send(fsend.at[to], frecv.at[t], sf_sem.at[n], rf_sem.at[n], (d, to)))
    frecv[t] = fsend[t]
    for copy in copies:
        copy.wait()
    for k in range(8):
        fd[k] = frecv[:, :, k, :].reshape(64, 128)


def project(act, grad, pin, pout, q, damp):
    sem = pltpu.SemaphoreType.DMA
    return pl.pallas_call(
        project_kernel,
        out_shape=(
            jax.ShapeDtypeStruct((8, 64, 128), F32),
            jax.ShapeDtypeStruct((16, 40, 128), F32),
        ),
        in_specs=[hbm(), hbm(), vmem(), vmem(), vmem(), vmem()],
        out_specs=(vmem(), vmem()),
        scratch_shapes=[
            pltpu.VMEM((4, 4, 128, 1024), F32),
            pltpu.VMEM((4, 4, 128, 1024), F32),
            pltpu.VMEM((1024, 256), BF16),
            pltpu.VMEM((1024, 256), BF16),
            pltpu.VMEM((4, 4, 128, 128), F32),
            pltpu.VMEM((4, 4, 128, 128), F32),
            pltpu.VMEM((3, 4, 128, 128), F32),
            pltpu.VMEM((3, 4, 128, 128), F32),
            pltpu.VMEM((3, 128, 128), F32),
            pltpu.VMEM((3, 128, 128), F32),
            pltpu.VMEM((3, 128, 128), F32),
            pltpu.VMEM((3, 128, 128), F32),
            pltpu.VMEM((16, 40, 128), F32),
            pltpu.VMEM((16, 4, 8, 128), F32),
            pltpu.VMEM((16, 4, 8, 128), F32),
            sem((2, 4)),
            sem((2, 3)),
            sem((2, 3)),
            sem((2, 3)),
            sem((2, 3)),
            sem((15,)),
            sem((15,)),
            sem((15,)),
            sem((15,)),
        ],
        compiler_params=params(1, 54),
    )(act, grad, pin, pout, q, damp)


def main_kernel(
    fd, qcols, qr, gram, back,
    rows, cols, slab, ch, cl, rh, rl, qg, pq, got_pq, fq_own, fq_got, fq, fp, got_fp, pt,
    sums, sums_all, damps, mine, bounds, out,
    s1, r1, sc, rc, sx, rx, s3, r3, s_pq, r_pq, s_fq, r_fq, s_fp, r_fp, s_sum, r_sum,
    s_bound, r_bound, s_out, r_out,
):
    d, t, z, c, x, y = place()
    dp_peers = [(shift(d, o, 8), t) for o in range(1, 8)]
    tensor_peers = [(d, shift(t, o, 16)) for o in range(1, 16)]
    xs = [(d, shift(x, o, 4) * 4 + y) for o in ORDER]
    ys = [(d, x * 4 + shift(y, o, 4)) for o in ORDER]
    greet(dp_peers + tensor_peers)
    greeted(22)
    slab_copies = [send(fd.at[peer[0]], slab.at[d], s1.at[n], r1.at[n], peer) for n, peer in enumerate(dp_peers)]
    zs = [send(fd, cols.at[d], sc.at[n], rc.at[n], (shift(z, o, 4) * 2 + c, t)) for n, o in enumerate(ORDER)]
    other = (z * 2 + 1 - c, t)
    cores = [send(fd, cols.at[d], sx.at[3], rx.at[3], other)]
    slab[d] = fd[d]
    cols[d] = fd[...]

    product = jnp.zeros((64, 512), F32)
    for k in range(4):
        value = jnp.concatenate((fd[2 * k], fd[2 * k + 1]), axis=1)
        high, low = parts(qcols[2 * k : 2 * k + 2].reshape(256, 512))
        product = product + few_rows(value, high, low, NN)
    turned = product.T
    for n in range(16):
        pq[n] = jnp.concatenate((turned[32 * n : 32 * n + 16], turned[32 * n + 16 : 32 * n + 32]), axis=1)

    for copy in slab_copies:
        copy.wait()
    for n in range(4):
        piece = slab[2 * n : 2 * n + 2].reshape(128, 128).T
        rows[t, 0, :, 128 * n : 128 * n + 128] = piece[:64]
        rows[t, 1, :, 128 * n : 128 * n + 128] = piece[64:]

    def hop(half, at, first, second, peer):
        return send(
            rows.at[at, half], rows.at[at, half], s3.at[half, first, second], r3.at[half, first, second], peer
        )

    firsts, rest = {}, []
    for n in range(3):
        firsts[0, n] = hop(0, t, n, 3, xs[n])
        firsts[1, n] = hop(1, t, n, 3, ys[n])
    pq_copies = [
        send(pq.at[peer[1]], got_pq.at[n], s_pq.at[n], r_pq.at[n], peer) for n, peer in enumerate(tensor_peers)
    ]
    for n in range(3):
        rest.append(hop(0, t, 3, n, ys[n]))
        rest.append(hop(1, t, 3, n, xs[n]))

    def source(half, p, n):
        back_by = jnp.where(n == 0, 3, jnp.where(n == 1, 1, jnp.where(n == 2, 2, 0)))
        if half == 0:
            return p * 4 + shift(y, back_by, 4)
        return shift(x, back_by, 4) * 4 + p

    sums[...] = jnp.zeros_like(sums)
    damps[...] = jnp.zeros_like(damps)
    for at in range(16):
        for half in range(2):
            lane = 64 * ((at // 4 if half == 0 else at % 4) % 2)
            damps[2 * at + half : 2 * at + half + 1, lane : lane + 64] = qr[at, 32:33, 64 * half : 64 * half + 64]
    for half in range(2):
        for n in range(4):
            qg[half, n] = jnp.concatenate(
                [qr[source(half, p, n), :, 64 * half : 64 * half + 64] for p in range(4)], axis=1
            )

    for n, o in enumerate(ORDER):
        firsts[0, n].wait()
        for m in range(3):
            rest.append(hop(0, shift(x, 4 - o, 4) * 4 + y, n, m, ys[m]))
        firsts[1, n].wait()
        for m in range(3):
            rest.append(hop(1, x * 4 + shift(y, 4 - o, 4), n, m, xs[m]))
    for copy in pq_copies:
        copy.wait()
    part = pq[t]
    for n in range(15):
        part = part + got_pq[n]
    fq_own[...] = part
    fq_copies = [send(fq_own, fq_got.at[d], s_fq.at[n], r_fq.at[n], peer) for n, peer in enumerate(dp_peers)]
    fq_got[d] = part
    for n, o in enumerate(ORDER):
        zs[n].wait()
        from_d = shift(z, 4 - o, 4) * 2 + c
        cores.append(send(cols.at[from_d], cols.at[from_d], sx.at[n], rx.at[n], other))
    for copy in fq_copies:
        copy.wait()
    for n in range(8):
        fq[:16, 64 * n : 64 * n + 64] = fq_got[n, :, :64]
        fq[16:, 64 * n : 64 * n + 64] = fq_got[n, :, 64:]
    fp[...] = jnp.zeros_like(fp)
    for copy in cores:
        copy.wait()

    def fill(n, carry):
        at = pl.ds(pl.multiple_of(n * 64, 64), 64)
        for k in range(8):
            high, low = parts(cols[n, k] * (1.0 / 512))
            ch[at, 128 * k : 128 * k + 128] = high
            cl[at, 128 * k : 128 * k + 128] = low
        return carry

    lax.fori_loop(0, 8, fill, 0)

    def group(half, n):
        sources = [source(half, p, n) for p in range(4)]
        high, low = parts(jnp.concatenate([rows[at, half] for at in sources], axis=0))
        rh[half, n] = high
        rl[half, n] = low
        total = jnp.zeros((256, 128), F32)
        for k in range(4):
            at = pl.ds(256 * k, 256)
            tile = mm(high, ch[:, at], NN) + mm(high, cl[:, at], NN) + mm(low, ch[:, at], NN)
            for p, source_at in enumerate(sources):
                down = pl.ds(pl.multiple_of(source_at * 128 + 64 * half, 64), 64)
                gram[down, 2 * k, :] = tile[64 * p : 64 * p + 64, :128]
                gram[down, 2 * k + 1, :] = tile[64 * p : 64 * p + 64, 128:]
            total = total + jnp.abs(tile[:, :128]) + jnp.abs(tile[:, 128:])
        for p in range(0, 4, 2):
            line = jnp.sum(total[64 * p : 64 * p + 128].T, axis=0, keepdims=True)
            sums[pl.ds(2 * sources[p] + half, 1), :64] = line[:, :64]
            sums[pl.ds(2 * sources[p + 1] + half, 1), 64:] = line[:, 64:]
        product = few_rows(fq[...], high, low, NT) * (1.0 / 512)
        value = product + qg[half, n, 32:33] * qg[half, n, :32]
        pt[half, n] = value
        fp[...] += few_rows(value, high, low, NN)

    group(0, 3)
    group(1, 3)

    def arrive(n, carry):
        for half in range(2):
            for first in range(4):
                at = source(half, 0, n)
                pltpu.make_async_remote_copy(
                    src_ref=rows.at[at, half],
                    dst_ref=rows.at[at, half],
                    send_sem=s3.at[half, first, n],
                    recv_sem=r3.at[half, first, n],
                    device_id=(d, t),
                    device_id_type=MESH,
                ).wait_recv()
            group(half, n)
        return carry

    lax.fori_loop(0, 3, arrive, 0)
    sum_copies = [
        send(sums, sums_all.at[n], s_sum.at[n], r_sum.at[n], peer) for n, peer in enumerate(tensor_peers)
    ]
    fp_copies = [send(fp, got_fp.at[n], s_fp.at[n], r_fp.at[n], peer) for n, peer in enumerate(dp_peers)]
    for copy in rest:
        copy.wait_send()
    for copy in sum_copies:
        copy.wait()
    row_sums = sums[...] + damps[...]
    for n in range(15):
        row_sums = row_sums + sums_all[n]
    high = jnp.max(row_sums, axis=(0, 1), keepdims=True)
    low = jnp.min(qr[:, 32:33].reshape(16, 128), axis=(0, 1), keepdims=True)
    mine[:8] = jnp.broadcast_to(high, (8, 128))
    mine[8:] = jnp.broadcast_to(low, (8, 128))
    bound_copies = [
        send(mine, bounds.at[n], s_bound.at[n], r_bound.at[n], peer) for n, peer in enumerate(dp_peers)
    ]
    for copy in fp_copies:
        copy.wait()
    fp_all = fp[...]
    for n in range(7):
        fp_all = fp_all + got_fp[n]
    for copy in bound_copies:
        copy.wait()
    bound_high, bound_low = mine[:1], mine[8:9]
    for n in range(7):
        bound_high = jnp.maximum(bound_high, bounds[n, :1])
        bound_low = jnp.minimum(bound_low, bounds[n, 8:9])
    bound_high = jnp.concatenate((bound_high, bound_high), axis=1)
    bound_low = jnp.concatenate((bound_low, bound_low), axis=1)
    ratio_low = bound_low / bound_high
    center = (1.0 + ratio_low) / 2.0
    half_width = (1.0 - ratio_low) / 2.0
    spread = center / half_width
    ratio = 1.0 / spread
    ratio_next = 1.0 / (2.0 * spread - ratio)
    keep = ratio_next * ratio
    add = 2.0 * ratio_next / half_width
    fp_all = fp_all / jnp.concatenate((bound_high, bound_high), axis=1)

    def finish(n, carry):
        for half in range(2):
            product = few_rows(fp_all, rh[half, n], rl[half, n], NT) * (1.0 / 512)
            query, damp = qg[half, n, :32], qg[half, n, 32:33]
            scaled = pt[half, n] / bound_high
            used = scaled / center
            first = query / center
            residual = query - used
            answer = first + (keep * first + add * residual)
            applied = (product / center + damp * used) / bound_high
            residual = residual - (keep * used + add * (scaled - applied))
            for p in range(4):
                at = source(half, p, n)
                lanes = slice(64 * half, 64 * half + 64)
                out[at, 0, :, lanes] = answer[:, 64 * p : 64 * p + 64]
                out[at, 1, :, lanes] = residual[:, 64 * p : 64 * p + 64]
        return carry

    lax.fori_loop(0, 4, finish, 0)
    copies = []
    for n in range(15):
        to = shift(t, n + 1, 16)
        copies.append(send(out.at[to], back.at[t], s_out.at[n], r_out.at[n], (d, to)))
    back[t] = out[t]

    for copy in copies:
        copy.wait()


def main(fd, qcols, qr):
    sem = pltpu.SemaphoreType.DMA
    return pl.pallas_call(
        main_kernel,
        out_shape=(
            jax.ShapeDtypeStruct((2048, 8, 128), F32),
            jax.ShapeDtypeStruct((16, 2, 32, 128), F32),
        ),
        in_specs=[vmem()] * 3,
        out_specs=(vmem(), vmem()),
        scratch_shapes=[
            pltpu.VMEM((16, 2, 64, 512), F32),
            pltpu.VMEM((8, 8, 64, 128), F32),
            pltpu.VMEM((8, 64, 128), F32),
            pltpu.VMEM((512, 1024), BF16),
            pltpu.VMEM((512, 1024), BF16),
            pltpu.VMEM((2, 4, 256, 512), BF16),
            pltpu.VMEM((2, 4, 256, 512), BF16),
            pltpu.VMEM((2, 4, 40, 256), F32),
            pltpu.VMEM((16, 16, 128), F32),
            pltpu.VMEM((15, 16, 128), F32),
            pltpu.VMEM((16, 128), F32),
            pltpu.VMEM((8, 16, 128), F32),
            pltpu.VMEM((32, 512), F32),
            pltpu.VMEM((32, 512), F32),
            pltpu.VMEM((7, 32, 512), F32),
            pltpu.VMEM((2, 4, 32, 256), F32),
            pltpu.VMEM((32, 128), F32),
            pltpu.VMEM((15, 32, 128), F32),
            pltpu.VMEM((32, 128), F32),
            pltpu.VMEM((16, 128), F32),
            pltpu.VMEM((7, 16, 128), F32),
            pltpu.VMEM((16, 2, 32, 128), F32),
            sem((7,)),
            sem((7,)),
            sem((3,)),
            sem((3,)),
            sem((4,)),
            sem((4,)),
            sem((2, 4, 4)),
            sem((2, 4, 4)),
            sem((15,)),
            sem((15,)),
            sem((7,)),
            sem((7,)),
            sem((7,)),
            sem((7,)),
            sem((15,)),
            sem((15,)),
            sem((7,)),
            sem((7,)),
            sem((15,)),
            sem((15,)),
        ],
        compiler_params=params(2, 36),
    )(fd, qcols, qr)


def finish_kernel(gram, back, out, sol, res, sem):
    copies = []
    for n in range(8):
        copy = pltpu.make_async_copy(gram.at[pl.ds(256 * n, 256)], out.at[pl.ds(256 * n, 256)], sem.at[n])
        copy.start()
        copies.append(copy)
    for n in range(4):
        sol[:, 128 * n : 128 * n + 128] = back[4 * n : 4 * n + 4, 0].reshape(128, 128).T
        res[:, 128 * n : 128 * n + 128] = back[4 * n : 4 * n + 4, 1].reshape(128, 128).T
    for copy in copies:
        copy.wait()


def finish(gram, back):
    return pl.pallas_call(
        finish_kernel,
        out_shape=(
            jax.ShapeDtypeStruct((2048, 8, 128), F32),
            jax.ShapeDtypeStruct((128, 512), F32),
            jax.ShapeDtypeStruct((128, 512), F32),
        ),
        in_specs=[vmem(), vmem()],
        out_specs=(hbm(), vmem(), vmem()),
        scratch_shapes=[pltpu.SemaphoreType.DMA((8,))],
        compiler_params=pltpu.CompilerParams(vmem_limit_bytes=16 * 2**20),
    )(gram, back)


def shards(activations, gradients, proj_in, proj_out, damping, queries):
    act = activations.reshape(4, 4, 128, 1024)
    grad = gradients.reshape(4, 4, 128, 1024)
    qcols = lax.all_gather(queries, "dp")
    fd, qr = project(act, grad, proj_in, proj_out, queries, damping.reshape(1, 128))
    gram, back = main(fd, qcols, qr)
    gram, answer, residual = finish(gram, back)
    return answer, residual, gram


def solution(mesh):
    return jax.shard_map(
        shards,
        mesh=mesh,
        in_specs=(
            P("dp", None, "tensor"),
            P("dp", None, "tensor"),
            P("tensor", None),
            P("tensor", None),
            P(("dp", "tensor")),
            P(("dp", "tensor"), None),
        ),
        out_specs=(P(("dp", "tensor"), None), P(("dp", "tensor"), None), P("dp", None, "tensor")),
        check_vma=False,
    )
```

time: 135 us -> 135 us (level)
  Pallas kernels: 130 us -> 116 us
  between operations: 0.67 us -> 14.1 us
    pallas_call x3 -> x2, Pallas kernels: 92.8 us -> 78.8 us  [the longest x1 74.6 us: main(): pl.pallas_call(main_kernel, out_shape=(jax.ShapeDtypeStruct((2048, 8, 128...]
  transfers between devices with their start and end apart: 0 -> 1, of which waited for: 0 -> 0; matrix products, arithmetic and copies ran while one was open for 0% -> 0% of each run, Pallas kernels for 0% -> 28%
where the time goes in v2:
time: 135 us
  Pallas kernels  116 us (86%)
  between operations  14.1 us (10%)
  local copies, waits for them, and re-layouts  3.51 us (3%)
    pallas_call x1, Pallas kernels, main(): pl.pallas_call(main_kernel, out_shape=(jax.ShapeDtypeStruct((2048, 8, 128...  74.6 us
    pallas_call x1, Pallas kernels, project(): pl.pallas_call(project_kernel, out_shape=(jax.ShapeDtypeStruct((8, 64, 12...  37.7 us
    pallas_call x1, Pallas kernels, finish(): pl.pallas_call(finish_kernel, out_shape=(jax.ShapeDtypeStruct((2048, 8, 1...  4.17 us
    unnamed x6, local copies, waits for them, and re-layouts  3.51 us
  transfers between devices with their start and end apart: 1, of which 0 were waited for; matrix products, arithmetic and copies ran while one was open for 0% of the time, Pallas kernels for 28%

profile of v2, /device:TPU:0, one launch (start us, length us, event | category | flops | bytes accessed | tf_op | source)
XLA Modules:
  0.0 134.8 jit_solution(17273817122733275173)
XLA Ops:
  7.2 0.0 all-gather.3.cloned.1.call-start
  7.2 0.7 all-gather.3.cloned.1.call-update
  7.9 37.7 %shard_map.85 = (f32[8,64,128]{2,1,0:T(8,128)}, f32[16,40,128]{2,1,0:T(8,128)}) custom-call(f32[4,4,128,1024]{3,2,1,0:T(8,128)} %bitcast.5, f32[4,4,128,1024]{3,2,1,0:T(8,128)} %bitcast.6, f32[1024,128]{1,0:T(8,128)} %pin.1, f32[1024,128]{1,0:T(8,128)} %pout.1, f32[128,512]{1,0:T(8,128)} %q.1, f32[1,128]{1,0:T(1,128)} %bitcast.7), custom_call_target="tpu_custom_call" | custom-call | tf_op jit(solution)/shard_map/pallas_call | solution.py:174
  45.6 0.0 all-gather.3.cloned.1.call-done
  45.6 0.0 copy-start
  45.6 1.6 %copy-done = f32[1024,512]{1,0:T(8,128)S(1)} copy-done((f32[1024,512]{1,0:T(8,128)S(1)}, f32[1024,512]{1,0:T(8,128)}, u32[]{:S(2)}) %copy-start) | copy-done | bytes 2097176
  47.2 0.0 copy-start.1
  47.2 1.0 copy-done.1
  48.2 0.0 copy-start.2
  48.2 0.9 copy-done.2
  49.1 74.6 %shard_map.86 = (f32[2048,8,128]{2,1,0:T(8,128)S(1)}, f32[16,2,32,128]{3,2,1,0:T(8,128)S(1)}) custom-call(f32[8,64,128]{2,1,0:T(8,128)S(1)} %copy-done.2, f32[8,128,512]{2,1,0:T(8,128)S(1)} %bitcast.4, f32[16,40,128]{2,1,0:T(8,128)S(1)} %copy-done.1), custom_call_target="tpu_custom_call" | custom-call | tf_op jit(solution)/shard_map/pallas_call | solution.py:435
  123.7 4.2 %shard_map.87 = (f32[2048,8,128]{2,1,0:T(8,128)}, f32[128,512]{1,0:T(8,128)}, f32[128,512]{1,0:T(8,128)}) custom-call(f32[2048,8,128]{2,1,0:T(8,128)S(1)} %get-tuple-element.12.gram, f32[16,2,32,128]{3,2,1,0:T(8,128)S(1)} %get-tuple-element.13.back), custom_call_target="tpu_custom_call" | custom-call | tf_op jit(solution)/shard_map/pallas_call | solution.py:505
Async XLA Ops:
  7.2 38.4 %all-gather.3.cloned.1.call-start = ((), (), s32[]{:S(2)}) async-start(), calls=%async_computation | async-start | bytes 2359296 | tf_op jit(solution)/shard_map/all_gather | solution.py:522
  45.6 1.6 %copy-start = (f32[1024,512]{1,0:T(8,128)S(1)}, f32[1024,512]{1,0:T(8,128)}, u32[]{:S(2)}) copy-start(f32[1024,512]{1,0:T(8,128)} %all-gather.3.cloned.1.call-done) | copy-start | bytes 6291460
  47.2 1.0 copy-start.1
  48.2 0.9 copy-start.2
Sparse Core Ops, SparseCore 0:
  9.7 27.8 all-gather.2

commit v3 on v2

--- a/solution.py
+++ b/solution.py
@@ -77,24 +77,40 @@
     return both[:rows] + both[rows:] + mm(high, weight_low, dims)
 
 
-def project_kernel(
-    act, grad, pin, pout, q, damp, fd, qr,
-    gbuf, abuf, wg, wa, yg, ya, r1g, r1a, s2g, s2a, r2g, r2a, qs, fsend, frecv,
-    in_sem, s1_sem, r1_sem, s2_sem, r2_sem, sq_sem, rq_sem, sf_sem, rf_sem,
+def main_kernel(
+    act, grad, pin_hbm, pout_hbm, q_hbm, damp_hbm, gram, back,
+    pin, pout, q, damp, gbuf, abuf, wg, wa, yg, ya, r1g, r1a, s2g, s2a, r2g, r2a, qs, qr, fsend, frecv, fd, qcols,
+    rows, cols, slab, ch, cl, rh, rl, qg, pq, got_pq, fq_own, fq_got, fq, fp, got_fp, fp_half, got_half, fp_total,
+    sums, sums_all, damps, mine, bounds, out, got_out,
+    small_sem, in_sem, s1_sem, r1_sem, s2_sem, r2_sem, sq_sem, rq_sem, sf_sem, rf_sem, sz_sem, rz_sem,
+    s1, r1, sc, rc, sx, rx, s3, r3, s_pq, r_pq, s_fq, r_fq, s_fp, r_fp, s_sum, r_sum,
+    s_bound, r_bound, s_out, r_out,
 ):
     d, t, z, c, x, y = place()
+    small = []
+    for n, (src, dst) in enumerate(((pout_hbm, pout), (pin_hbm, pin), (q_hbm, q), (damp_hbm, damp))):
+        copy = pltpu.make_async_copy(src, dst, small_sem.at[n])
+        copy.start()
+        small.append(copy)
     loads = []
     for n, o in enumerate(ORDER + (0,)):
         g = pltpu.make_async_copy(grad.at[shift(x, o, 4)], gbuf.at[n], in_sem.at[0, n])
         a = pltpu.make_async_copy(act.at[:, shift(y, o, 4)], abuf.at[n], in_sem.at[1, n])
-        g.start()
-        a.start()
+        if n < 2:
+            g.start()
+            a.start()
         loads.append((g, a))
-    peers = [(d, shift(t, o, 16)) for o in range(1, 16)]
-    greet(peers)
+    dp_peers = [(shift(d, o, 8), t) for o in range(1, 8)]
+    tensor_peers = [(d, shift(t, o, 16)) for o in range(1, 16)]
+    xs = [(d, shift(x, o, 4) * 4 + y) for o in ORDER]
+    ys = [(d, x * 4 + shift(y, o, 4)) for o in ORDER]
+    other = (z * 2 + 1 - c, t)
+    greet(dp_peers + tensor_peers)
     row = lax.broadcasted_iota(jnp.int32, (128, 128), 0)
     column = lax.broadcasted_iota(jnp.int32, (128, 128), 1)
     order = (row == 16 * lax.rem(column, 8) + lax.div(column, 8)).astype(BF16)
+    for copy in small:
+        copy.wait()
     high, low = parts(pout[...])
     wg[:, :128] = mm(high, order, NN).astype(BF16)
     wg[:, 128:] = mm(low, order, NN).astype(BF16)
@@ -104,8 +120,11 @@
     for n in range(16):
         qs[n, :32] = q[:, pl.ds(128 * (n // 4), 128)].T[32 * (n % 4) : 32 * (n % 4) + 32]
         qs[n, 32:] = jnp.broadcast_to(damp[...], (8, 128))
-    greeted(15)
+    qcols[d] = q[...]
+    greeted(22)
     copies = []
+    q_zs = [send(q, qcols.at[d], sz_sem.at[n], rz_sem.at[n], (shift(z, o, 4) * 2 + c, t)) for n, o in enumerate(ORDER)]
+    q_cores = [send(q, qcols.at[d], sz_sem.at[6], rz_sem.at[6], other)]
     for n in range(15):
         to = shift(t, n + 1, 16)
         copies.append(send(qs.at[to], qr.at[t], sq_sem.at[n], rq_sem.at[n], (d, to)))
@@ -113,23 +132,28 @@
 
     def project(buf, weight, out, n):
         def step(m, carry):
-            high, low = parts(buf[n, m])
+            at = pl.ds(2 * m, 2)
+            high, low = parts(buf[n, at].reshape(256, 1024))
             first = mm(high, weight[...], NN)
             second = mm(low, weight[:, :128], NN)
-            out[n, m] = first[:, :128] + first[:, 128:] + second
+            out[n, at] = (first[:, :128] + first[:, 128:] + second).reshape(2, 128, 128)
             return carry
 
-        lax.fori_loop(0, 4, step, 0)
+        lax.fori_loop(0, 2, step, 0)
 
     firsts = []
     for n, o in enumerate(ORDER + (0,)):
         loads[n][0].wait()
+        if n < 2:
+            loads[n + 2][0].start()
         project(gbuf, wg, yg, n)
         if o:
             firsts.append(
                 send(yg.at[n], r1g.at[n], s1_sem.at[0, n], r1_sem.at[0, n], (d, shift(x, o, 4) * 4 + y))
             )
         loads[n][1].wait()
+        if n < 2:
+            loads[n + 2][1].start()
         project(abuf, wa, ya, n)
         if o:
             firsts.append(
@@ -163,73 +187,22 @@
         to = shift(t, n + 1, 16)
         copies.append(send(fsend.at[to], frecv.at[t], sf_sem.at[n], rf_sem.at[n], (d, to)))
     frecv[t] = fsend[t]
+    for n, o in enumerate(ORDER):
+        q_zs[n].wait()
+        from_d = shift(z, 4 - o, 4) * 2 + c
+        q_cores.append(send(qcols.at[from_d], qcols.at[from_d], sz_sem.at[3 + n], rz_sem.at[3 + n], other))
     for copy in copies:
         copy.wait()
     for k in range(8):
         fd[k] = frecv[:, :, k, :].reshape(64, 128)
-
-
-def project(act, grad, pin, pout, q, damp):
-    sem = pltpu.SemaphoreType.DMA
-    return pl.pallas_call(
-        project_kernel,
-        out_shape=(
-            jax.ShapeDtypeStruct((8, 64, 128), F32),
-            jax.ShapeDtypeStruct((16, 40, 128), F32),
-        ),
-        in_specs=[hbm(), hbm(), vmem(), vmem(), vmem(), vmem()],
-        out_specs=(vmem(), vmem()),
-        scratch_shapes=[
-            pltpu.VMEM((4, 4, 128, 1024), F32),
-            pltpu.VMEM((4, 4, 128, 1024), F32),
-            pltpu.VMEM((1024, 256), BF16),
-            pltpu.VMEM((1024, 256), BF16),
-            pltpu.VMEM((4, 4, 128, 128), F32),
-            pltpu.VMEM((4, 4, 128, 128), F32),
-            pltpu.VMEM((3, 4, 128, 128), F32),
-            pltpu.VMEM((3, 4, 128, 128), F32),
-            pltpu.VMEM((3, 128, 128), F32),
-            pltpu.VMEM((3, 128, 128), F32),
-            pltpu.VMEM((3, 128, 128), F32),
-            pltpu.VMEM((3, 128, 128), F32),
-            pltpu.VMEM((16, 40, 128), F32),
-            pltpu.VMEM((16, 4, 8, 128), F32),
-            pltpu.VMEM((16, 4, 8, 128), F32),
-            sem((2, 4)),
-            sem((2, 3)),
-            sem((2, 3)),
-            sem((2, 3)),
-            sem((2, 3)),
-            sem((15,)),
-            sem((15,)),
-            sem((15,)),
-            sem((15,)),
-        ],
-        compiler_params=params(1, 54),
-    )(act, grad, pin, pout, q, damp)
-
-
-def main_kernel(
-    fd, qcols, qr, gram, back,
-    rows, cols, slab, ch, cl, rh, rl, qg, pq, got_pq, fq_own, fq_got, fq, fp, got_fp, pt,
-    sums, sums_all, damps, mine, bounds, out,
-    s1, r1, sc, rc, sx, rx, s3, r3, s_pq, r_pq, s_fq, r_fq, s_fp, r_fp, s_sum, r_sum,
-    s_bound, r_bound, s_out, r_out,
-):
-    d, t, z, c, x, y = place()
-    dp_peers = [(shift(d, o, 8), t) for o in range(1, 8)]
-    tensor_peers = [(d, shift(t, o, 16)) for o in range(1, 16)]
-    xs = [(d, shift(x, o, 4) * 4 + y) for o in ORDER]
-    ys = [(d, x * 4 + shift(y, o, 4)) for o in ORDER]
-    greet(dp_peers + tensor_peers)
-    greeted(22)
     slab_copies = [send(fd.at[peer[0]], slab.at[d], s1.at[n], r1.at[n], peer) for n, peer in enumerate(dp_peers)]
     zs = [send(fd, cols.at[d], sc.at[n], rc.at[n], (shift(z, o, 4) * 2 + c, t)) for n, o in enumerate(ORDER)]
-    other = (z * 2 + 1 - c, t)
     cores = [send(fd, cols.at[d], sx.at[3], rx.at[3], other)]
     slab[d] = fd[d]
     cols[d] = fd[...]
 
+    for copy in q_cores:
+        copy.wait()
     product = jnp.zeros((64, 512), F32)
     for k in range(4):
         value = jnp.concatenate((fd[2 * k], fd[2 * k + 1]), axis=1)
@@ -246,27 +219,55 @@
         rows[t, 0, :, 128 * n : 128 * n + 128] = piece[:64]
         rows[t, 1, :, 128 * n : 128 * n + 128] = piece[64:]
 
-    def hop(half, at, first, second, peer):
-        return send(
-            rows.at[at, half], rows.at[at, half], s3.at[half, first, second], r3.at[half, first, second], peer
+    def device(half, first, second):
+        if half == 0:
+            return shift(x, first % 4, 4) * 4 + shift(y, second % 4, 4)
+        return shift(x, second % 4, 4) * 4 + shift(y, first % 4, 4)
+
+    def message(half, first, second, part, axis, step):
+        at = device(half, first, second)
+        to = device(half, step, 0) if axis == 0 else device(half, 0, step)
+        seen = ((first - step) % 4, second % 4) if axis == 0 else (first % 4, (second - step) % 4)
+        ref = rows.at[at, half] if part is None else rows.at[at, half, pl.ds(32 * part, 32)]
+        return pltpu.make_async_remote_copy(
+            src_ref=ref,
+            dst_ref=ref,
+            send_sem=s3.at[half, seen[0], seen[1], part or 0],
+            recv_sem=r3.at[half, seen[0], seen[1], part or 0],
+            device_id=(d, to),
+            device_id_type=MESH,
         )
 
-    firsts, rest = {}, []
-    for n in range(3):
-        firsts[0, n] = hop(0, t, n, 3, xs[n])
-        firsts[1, n] = hop(1, t, n, 3, ys[n])
+    rest = []
+
+    def pass_on(half, first, second, part, axis, *steps):
+        for step in steps:
+            copy = message(half, first, second, part, axis, step)
+            copy.start()
+            rest.append(copy)
+
+    def arrived(half, first, second, part):
+        at = device(half, first, second)
+        ref = rows.at[at, half] if part is None else rows.at[at, half, pl.ds(32 * part, 32)]
+        pltpu.make_async_remote_copy(
+            src_ref=ref,
+            dst_ref=ref,
+            send_sem=s3.at[half, first % 4, second % 4, part or 0],
+            recv_sem=r3.at[half, first % 4, second % 4, part or 0],
+            device_id=(d, t),
+            device_id_type=MESH,
+        ).wait_recv()
+
+    for axis in range(2):
+        for half in range(2):
+            pass_on(half, 0, 0, None, axis, 1, -1)
     pq_copies = [
         send(pq.at[peer[1]], got_pq.at[n], s_pq.at[n], r_pq.at[n], peer) for n, peer in enumerate(tensor_peers)
     ]
-    for n in range(3):
-        rest.append(hop(0, t, 3, n, ys[n]))
-        rest.append(hop(1, t, 3, n, xs[n]))
-
     def source(half, p, n):
-        back_by = jnp.where(n == 0, 3, jnp.where(n == 1, 1, jnp.where(n == 2, 2, 0)))
         if half == 0:
-            return p * 4 + shift(y, back_by, 4)
-        return shift(x, back_by, 4) * 4 + p
+            return p * 4 + shift(y, n, 4)
+        return shift(x, n, 4) * 4 + p
 
     sums[...] = jnp.zeros_like(sums)
     damps[...] = jnp.zeros_like(damps)
@@ -280,13 +281,19 @@
                 [qr[source(half, p, n), :, 64 * half : 64 * half + 64] for p in range(4)], axis=1
             )
 
-    for n, o in enumerate(ORDER):
-        firsts[0, n].wait()
-        for m in range(3):
-            rest.append(hop(0, shift(x, 4 - o, 4) * 4 + y, n, m, ys[m]))
-        firsts[1, n].wait()
-        for m in range(3):
-            rest.append(hop(1, x * 4 + shift(y, 4 - o, 4), n, m, xs[m]))
+    for first in (-1, 1):
+        for half in range(2):
+            arrived(half, first, 0, None)
+            pass_on(half, first, 0, 0 if first < 0 else 1, 0, -first)
+            pass_on(half, first, 0, None, 1, 1, -1)
+    for second in (-1, 1):
+        for half in range(2):
+            arrived(half, 0, second, None)
+            pass_on(half, 0, second, 0 if second < 0 else 1, 1, -second)
+    for part in range(2):
+        for half in range(2):
+            arrived(half, 2, 0, part)
+            pass_on(half, 2, 0, part, 1, 1, -1)
     for copy in pq_copies:
         copy.wait()
     part = pq[t]
@@ -299,6 +306,11 @@
         zs[n].wait()
         from_d = shift(z, 4 - o, 4) * 2 + c
         cores.append(send(cols.at[from_d], cols.at[from_d], sx.at[n], rx.at[n], other))
+    for first in (-1, 1):
+        for second in (-1, 1):
+            for half in range(2):
+                arrived(half, first, second, None)
+                pass_on(half, first, second, 0 if second < 0 else 1, 1, -second)
     for copy in fq_copies:
         copy.wait()
     for n in range(8):
@@ -338,34 +350,46 @@
             sums[pl.ds(2 * sources[p + 1] + half, 1), 64:] = line[:, 64:]
         product = few_rows(fq[...], high, low, NT) * (1.0 / 512)
         value = product + qg[half, n, 32:33] * qg[half, n, :32]
-        pt[half, n] = value
+        for p, at in enumerate(sources):
+            out[0, at, :, 64 * half : 64 * half + 64] = value[:, 64 * p : 64 * p + 64]
         fp[...] += few_rows(value, high, low, NN)
 
-    group(0, 3)
-    group(1, 3)
-
-    def arrive(n, carry):
-        for half in range(2):
-            for first in range(4):
-                at = source(half, 0, n)
-                pltpu.make_async_remote_copy(
-                    src_ref=rows.at[at, half],
-                    dst_ref=rows.at[at, half],
-                    send_sem=s3.at[half, first, n],
-                    recv_sem=r3.at[half, first, n],
-                    device_id=(d, t),
-                    device_id_type=MESH,
-                ).wait_recv()
-            group(half, n)
-        return carry
-
-    lax.fori_loop(0, 3, arrive, 0)
+    def groups(first_step, last_step):
+        def step(n, carry):
+            group(0, n)
+            group(1, n)
+            return carry
+
+        lax.fori_loop(first_step, last_step, step, 0)
+
+    for second in (-1, 1):
+        for part in range(2):
+            for half in range(2):
+                arrived(half, 2, second, part)
+                if part == (0 if second < 0 else 1):
+                    pass_on(half, 2, second, part, 1, -second)
+    groups(0, 2)
+    groups(3, 4)
+    for first in (0, -1, 1, 2):
+        for part in range(2):
+            for half in range(2):
+                arrived(half, first, 2, part)
+    groups(2, 3)
+    fp_core = send(fp, got_fp, s_fp.at[0], r_fp.at[0], other)
     sum_copies = [
         send(sums, sums_all.at[n], s_sum.at[n], r_sum.at[n], peer) for n, peer in enumerate(tensor_peers)
     ]
-    fp_copies = [send(fp, got_fp.at[n], s_fp.at[n], r_fp.at[n], peer) for n, peer in enumerate(dp_peers)]
-    for copy in rest:
-        copy.wait_send()
+    fp_core.wait()
+    own_half = pl.ds(pl.multiple_of(16 * c, 16), 16)
+    fp_half[...] = fp[own_half] + got_fp[own_half]
+    fp_zs = [
+        send(fp_half, got_half.at[n], s_fp.at[1 + n], r_fp.at[1 + n], (shift(z, o, 4) * 2 + c, t))
+        for n, o in enumerate(ORDER)
+    ]
+    copies = []
+    for n, peer in enumerate(tensor_peers):
+        copies.append(send(out.at[0, peer[1]], got_out.at[0, t], s_out.at[0, n], r_out.at[0, n], peer))
+    got_out[0, t] = out[0, t]
     for copy in sum_copies:
         copy.wait()
     row_sums = sums[...] + damps[...]
@@ -378,19 +402,33 @@
     bound_copies = [
         send(mine, bounds.at[n], s_bound.at[n], r_bound.at[n], peer) for n, peer in enumerate(dp_peers)
     ]
-    for copy in fp_copies:
-        copy.wait()
-    fp_all = fp[...]
-    for n in range(7):
-        fp_all = fp_all + got_fp[n]
+    for copy in fp_zs:
+        copy.wait()
+    fp_total[own_half] = fp_half[...] + got_half[0] + (got_half[1] + got_half[2])
+    fp_core = send(fp_total.at[own_half], fp_total.at[own_half], s_fp.at[4], r_fp.at[4], other)
+    fp_core.wait()
+    fp_all = fp_total[...]
+    row_bound = mine[:1]
+    fp_all = fp_all * (1.0 / 512) / jnp.concatenate([row_bound] * 4, axis=1)
+
+    def finish(n, carry):
+        for half in range(2):
+            product = few_rows(fp_all, rh[half, n], rl[half, n], NT)
+            for p in range(4):
+                out[1, source(half, p, n), :, 64 * half : 64 * half + 64] = product[:, 64 * p : 64 * p + 64]
+        return carry
+
+    lax.fori_loop(0, 4, finish, 0)
+    for n, peer in enumerate(tensor_peers):
+        copies.append(send(out.at[1, peer[1]], got_out.at[1, t], s_out.at[1, n], r_out.at[1, n], peer))
+    got_out[1, t] = out[1, t]
     for copy in bound_copies:
         copy.wait()
-    bound_high, bound_low = mine[:1], mine[8:9]
+    bound_high, bound_low = row_bound, mine[8:9]
     for n in range(7):
         bound_high = jnp.maximum(bound_high, bounds[n, :1])
         bound_low = jnp.minimum(bound_low, bounds[n, 8:9])
-    bound_high = jnp.concatenate((bound_high, bound_high), axis=1)
-    bound_low = jnp.concatenate((bound_low, bound_low), axis=1)
+    row_share = row_bound / bound_high
     ratio_low = bound_low / bound_high
     center = (1.0 + ratio_low) / 2.0
     half_width = (1.0 - ratio_low) / 2.0
@@ -399,38 +437,26 @@
     ratio_next = 1.0 / (2.0 * spread - ratio)
     keep = ratio_next * ratio
     add = 2.0 * ratio_next / half_width
-    fp_all = fp_all / jnp.concatenate((bound_high, bound_high), axis=1)
-
-    def finish(n, carry):
-        for half in range(2):
-            product = few_rows(fp_all, rh[half, n], rl[half, n], NT) * (1.0 / 512)
-            query, damp = qg[half, n, :32], qg[half, n, 32:33]
-            scaled = pt[half, n] / bound_high
-            used = scaled / center
-            first = query / center
-            residual = query - used
-            answer = first + (keep * first + add * residual)
-            applied = (product / center + damp * used) / bound_high
-            residual = residual - (keep * used + add * (scaled - applied))
-            for p in range(4):
-                at = source(half, p, n)
-                lanes = slice(64 * half, 64 * half + 64)
-                out[at, 0, :, lanes] = answer[:, 64 * p : 64 * p + 64]
-                out[at, 1, :, lanes] = residual[:, 64 * p : 64 * p + 64]
+    for copy in rest:
+        copy.wait_send()
+    for copy in copies:
+        copy.wait()
+
+    def combine(n, carry):
+        query, damp_row = qs[n, :32], qs[n, 32:33]
+        scaled = got_out[0, n] / bound_high
+        used = scaled / center
+        first = query / center
+        residual = query - used
+        back[n, 0] = first + (keep * first + add * residual)
+        applied = got_out[1, n] * row_share / center + damp_row * used
+        back[n, 1] = residual - (keep * used + add * (scaled - applied / bound_high))
         return carry
 
-    lax.fori_loop(0, 4, finish, 0)
-    copies = []
-    for n in range(15):
-        to = shift(t, n + 1, 16)
-        copies.append(send(out.at[to], back.at[t], s_out.at[n], r_out.at[n], (d, to)))
-    back[t] = out[t]
-
-    for copy in copies:
-        copy.wait()
-
-
-def main(fd, qcols, qr):
+    lax.fori_loop(0, 16, combine, 0)
+
+
+def main(act, grad, pin, pout, q, damp):
     sem = pltpu.SemaphoreType.DMA
     return pl.pallas_call(
         main_kernel,
@@ -438,9 +464,31 @@
             jax.ShapeDtypeStruct((2048, 8, 128), F32),
             jax.ShapeDtypeStruct((16, 2, 32, 128), F32),
         ),
-        in_specs=[vmem()] * 3,
+        in_specs=[hbm()] * 6,
         out_specs=(vmem(), vmem()),
         scratch_shapes=[
+            pltpu.VMEM((1024, 128), F32),
+            pltpu.VMEM((1024, 128), F32),
+            pltpu.VMEM((128, 512), F32),
+            pltpu.VMEM((1, 128), F32),
+            pltpu.VMEM((4, 4, 128, 1024), F32),
+            pltpu.VMEM((4, 4, 128, 1024), F32),
+            pltpu.VMEM((1024, 256), BF16),
+            pltpu.VMEM((1024, 256), BF16),
+            pltpu.VMEM((4, 4, 128, 128), F32),
+            pltpu.VMEM((4, 4, 128, 128), F32),
+            pltpu.VMEM((3, 4, 128, 128), F32),
+            pltpu.VMEM((3, 4, 128, 128), F32),
+            pltpu.VMEM((3, 128, 128), F32),
+            pltpu.VMEM((3, 128, 128), F32),
+            pltpu.VMEM((3, 128, 128), F32),
+            pltpu.VMEM((3, 128, 128), F32),
+            pltpu.VMEM((16, 40, 128), F32),
+            pltpu.VMEM((16, 40, 128), F32),
+            pltpu.VMEM((16, 4, 8, 128), F32),
+            pltpu.VMEM((16, 4, 8, 128), F32),
+            pltpu.VMEM((8, 64, 128), F32),
+            pltpu.VMEM((8, 128, 512), F32),
             pltpu.VMEM((16, 2, 64, 512), F32),
             pltpu.VMEM((8, 8, 64, 128), F32),
             pltpu.VMEM((8, 64, 128), F32),
@@ -455,37 +503,52 @@
             pltpu.VMEM((8, 16, 128), F32),
             pltpu.VMEM((32, 512), F32),
             pltpu.VMEM((32, 512), F32),
-            pltpu.VMEM((7, 32, 512), F32),
-            pltpu.VMEM((2, 4, 32, 256), F32),
+            pltpu.VMEM((32, 512), F32),
+            pltpu.VMEM((16, 512), F32),
+            pltpu.VMEM((3, 16, 512), F32),
+            pltpu.VMEM((32, 512), F32),
             pltpu.VMEM((32, 128), F32),
             pltpu.VMEM((15, 32, 128), F32),
             pltpu.VMEM((32, 128), F32),
             pltpu.VMEM((16, 128), F32),
             pltpu.VMEM((7, 16, 128), F32),
-            pltpu.VMEM((16, 2, 32, 128), F32),
+            pltpu.VMEM((2, 16, 32, 128), F32),
+            pltpu.VMEM((2, 16, 32, 128), F32),
+            sem((4,)),
+            sem((2, 4)),
+            sem((2, 3)),
+            sem((2, 3)),
+            sem((2, 3)),
+            sem((2, 3)),
+            sem((15,)),
+            sem((15,)),
+            sem((15,)),
+            sem((15,)),
+            sem((7,)),
+            sem((7,)),
             sem((7,)),
             sem((7,)),
             sem((3,)),
             sem((3,)),
             sem((4,)),
             sem((4,)),
-            sem((2, 4, 4)),
-            sem((2, 4, 4)),
-            sem((15,)),
-            sem((15,)),
-            sem((7,)),
-            sem((7,)),
-            sem((7,)),
-            sem((7,)),
-            sem((15,)),
-            sem((15,)),
-            sem((7,)),
-            sem((7,)),
-            sem((15,)),
-            sem((15,)),
+            sem((2, 4, 4, 2)),
+            sem((2, 4, 4, 2)),
+            sem((15,)),
+            sem((15,)),
+            sem((7,)),
+            sem((7,)),
+            sem((7,)),
+            sem((7,)),
+            sem((15,)),
+            sem((15,)),
+            sem((7,)),
+            sem((7,)),
+            sem((2, 15)),
+            sem((2, 15)),
         ],
-        compiler_params=params(2, 36),
-    )(fd, qcols, qr)
+        compiler_params=params(1, 44),
+    )(act, grad, pin, pout, q, damp)
 
 
 def finish_kernel(gram, back, out, sol, res, sem):
@@ -519,9 +582,7 @@
 def shards(activations, gradients, proj_in, proj_out, damping, queries):
     act = activations.reshape(4, 4, 128, 1024)
     grad = gradients.reshape(4, 4, 128, 1024)
-    qcols = lax.all_gather(queries, "dp")
-    fd, qr = project(act, grad, proj_in, proj_out, queries, damping.reshape(1, 128))
-    gram, back = main(fd, qcols, qr)
+    gram, back = main(act, grad, proj_in, proj_out, queries, damping.reshape(1, 128))
     gram, answer, residual = finish(gram, back)
     return answer, residual, gram
 

time: 135 us -> 108 us (0.80)
  between operations: 14.1 us -> 0.81 us
  Pallas kernels: 116 us -> 103 us
    pallas_call x1 -> x0, Pallas kernels: 37.7 us -> none  [project(): pl.pallas_call(project_kernel, out_shape=(jax.ShapeDtypeStruct((8, 64, 12...]
    pallas_call x1, Pallas kernels: 74.6 us -> 98.9 us  [main(): pl.pallas_call(main_kernel, out_shape=(jax.ShapeDtypeStruct((2048, 8, 128...]
    unnamed x6 -> x8, local copies, waits for them, and re-layouts: 3.51 us -> 3.68 us
  transfers between devices with their start and end apart: 1 -> 0, of which waited for: 0 -> 0; matrix products, arithmetic and copies ran while one was open for 0% -> 0% of each run, Pallas kernels for 28% -> 0%
where the time goes in v3:
time: 108 us
  Pallas kernels  103 us (95%)
  local copies, waits for them, and re-layouts  3.68 us (3%)
    pallas_call x1, Pallas kernels, main(): pl.pallas_call(main_kernel, out_shape=(jax.ShapeDtypeStruct((2048, 8, 128...  98.9 us
    pallas_call x1, Pallas kernels, finish(): pl.pallas_call(finish_kernel, out_shape=(jax.ShapeDtypeStruct((2048, 8, 1...  4.17 us
    unnamed x8, local copies, waits for them, and re-layouts  3.68 us

profile of v3, /device:TPU:0, one launch (start us, length us, event | category | flops | bytes accessed | tf_op | source)
XLA Modules:
  0.0 107.5 jit_solution(14783790479226751450)
XLA Ops:
  0.6 0.0 copy-start
  0.6 1.0 copy-done
  1.7 0.0 copy-start.1
  1.7 1.0 copy-done.1
  2.7 0.0 copy-start.2
  2.7 0.9 copy-done.2
  3.7 0.0 copy-start.3
  3.7 0.7 copy-done.3
  4.3 98.9 %shard_map.85 = (f32[2048,8,128]{2,1,0:T(8,128)S(1)}, f32[16,2,32,128]{3,2,1,0:T(8,128)S(1)}) custom-call(f32[4,4,128,1024]{3,2,1,0:T(8,128)} %bitcast.4, f32[4,4,128,1024]{3,2,1,0:T(8,128)} %bitcast.5, f32[1024,128]{1,0:T(8,128)S(1)} %copy-done, f32[1024,128]{1,0:T(8,128)S(1)} %copy-done.1, f32[128,512]{1,0:T(8,128)S(1)} %copy-done.2, f32[1,128]{1,0:T(1,128)S(1)} %bitcast.3), custom_call_target="tpu_custom_call" | custom-call | tf_op jit(solution)/shard_map/pallas_call | solution.py:461
  103.2 4.2 %shard_map.86 = (f32[2048,8,128]{2,1,0:T(8,128)}, f32[128,512]{1,0:T(8,128)}, f32[128,512]{1,0:T(8,128)}) custom-call(f32[2048,8,128]{2,1,0:T(8,128)S(1)} %get-tuple-element.8.gram, f32[16,2,32,128]{3,2,1,0:T(8,128)S(1)} %get-tuple-element.9.back), custom_call_target="tpu_custom_call" | custom-call | tf_op jit(solution)/shard_map/pallas_call | solution.py:568
Async XLA Ops:
  0.6 1.0 copy-start
  1.7 1.0 copy-start.1
  2.7 0.9 copy-start.2
  3.7 0.7 copy-start.3

commit v4 on v3

--- a/solution.py
+++ b/solution.py
@@ -125,10 +125,6 @@
     copies = []
     q_zs = [send(q, qcols.at[d], sz_sem.at[n], rz_sem.at[n], (shift(z, o, 4) * 2 + c, t)) for n, o in enumerate(ORDER)]
     q_cores = [send(q, qcols.at[d], sz_sem.at[6], rz_sem.at[6], other)]
-    for n in range(15):
-        to = shift(t, n + 1, 16)
-        copies.append(send(qs.at[to], qr.at[t], sq_sem.at[n], rq_sem.at[n], (d, to)))
-    qr[t] = qs[t]
 
     def project(buf, weight, out, n):
         def step(m, carry):
@@ -159,21 +155,27 @@
             firsts.append(
                 send(ya.at[n], r1a.at[n], s1_sem.at[1, n], r1_sem.at[1, n], (d, x * 4 + shift(y, o, 4)))
             )
-    for copy in firsts:
-        copy.wait()
 
     def total(own, got, at):
         return own[3, at] + got[0, at] + (got[1, at] + got[2, at])
 
     seconds = []
+    for copy in firsts[::2]:
+        copy.wait_recv()
     for n, o in enumerate(ORDER):
-        yy, xx = shift(y, o, 4), shift(x, o, 4)
+        yy = shift(y, o, 4)
         s2g[n] = total(yg, r1g, yy)
         seconds.append(send(s2g.at[n], r2g.at[n], s2_sem.at[0, n], r2_sem.at[0, n], (d, x * 4 + yy)))
+    for copy in firsts[1::2]:
+        copy.wait_recv()
+    for n, o in enumerate(ORDER):
+        xx = shift(x, o, 4)
         s2a[n] = total(ya, r1a, xx)
         seconds.append(send(s2a.at[n], r2a.at[n], s2_sem.at[1, n], r2_sem.at[1, n], (d, xx * 4 + y)))
     pg = total(yg, r1g, y)
     pa = total(ya, r1a, x)
+    for copy in firsts:
+        copy.wait_send()
     for copy in seconds:
         copy.wait()
     pg = pg + r2g[0] + (r2g[1] + r2g[2])
@@ -195,9 +197,14 @@
         copy.wait()
     for k in range(8):
         fd[k] = frecv[:, :, k, :].reshape(64, 128)
+    query_copies = []
     slab_copies = [send(fd.at[peer[0]], slab.at[d], s1.at[n], r1.at[n], peer) for n, peer in enumerate(dp_peers)]
     zs = [send(fd, cols.at[d], sc.at[n], rc.at[n], (shift(z, o, 4) * 2 + c, t)) for n, o in enumerate(ORDER)]
     cores = [send(fd, cols.at[d], sx.at[3], rx.at[3], other)]
+    for n in range(15):
+        to = shift(t, n + 1, 16)
+        query_copies.append(send(qs.at[to], qr.at[t], sq_sem.at[n], rq_sem.at[n], (d, to)))
+    qr[t] = qs[t]
     slab[d] = fd[d]
     cols[d] = fd[...]
 
@@ -269,6 +276,8 @@
             return p * 4 + shift(y, n, 4)
         return shift(x, n, 4) * 4 + p
 
+    for copy in query_copies:
+        copy.wait()
     sums[...] = jnp.zeros_like(sums)
     damps[...] = jnp.zeros_like(damps)
     for at in range(16):
@@ -306,17 +315,6 @@
         zs[n].wait()
         from_d = shift(z, 4 - o, 4) * 2 + c
         cores.append(send(cols.at[from_d], cols.at[from_d], sx.at[n], rx.at[n], other))
-    for first in (-1, 1):
-        for second in (-1, 1):
-            for half in range(2):
-                arrived(half, first, second, None)
-                pass_on(half, first, second, 0 if second < 0 else 1, 1, -second)
-    for copy in fq_copies:
-        copy.wait()
-    for n in range(8):
-        fq[:16, 64 * n : 64 * n + 64] = fq_got[n, :, :64]
-        fq[16:, 64 * n : 64 * n + 64] = fq_got[n, :, 64:]
-    fp[...] = jnp.zeros_like(fp)
     for copy in cores:
         copy.wait()
 
@@ -348,33 +346,59 @@
             line = jnp.sum(total[64 * p : 64 * p + 128].T, axis=0, keepdims=True)
             sums[pl.ds(2 * sources[p] + half, 1), :64] = line[:, :64]
             sums[pl.ds(2 * sources[p + 1] + half, 1), 64:] = line[:, 64:]
+
+    def queries_of(half, n):
+        sources = [source(half, p, n) for p in range(4)]
+        high, low = rh[half, n], rl[half, n]
         product = few_rows(fq[...], high, low, NT) * (1.0 / 512)
         value = product + qg[half, n, 32:33] * qg[half, n, :32]
         for p, at in enumerate(sources):
             out[0, at, :, 64 * half : 64 * half + 64] = value[:, 64 * p : 64 * p + 64]
         fp[...] += few_rows(value, high, low, NN)
 
-    def groups(first_step, last_step):
-        def step(n, carry):
-            group(0, n)
-            group(1, n)
-            return carry
-
-        lax.fori_loop(first_step, last_step, step, 0)
-
-    for second in (-1, 1):
+    def pass_third(first):
+        for second in (-1, 1):
+            for half in range(2):
+                arrived(half, first, second, None)
+                pass_on(half, first, second, 0 if second < 0 else 1, 1, -second)
+
+    def pass_fourth(second):
         for part in range(2):
             for half in range(2):
                 arrived(half, 2, second, part)
                 if part == (0 if second < 0 else 1):
                     pass_on(half, 2, second, part, 1, -second)
-    groups(0, 2)
-    groups(3, 4)
-    for first in (0, -1, 1, 2):
-        for part in range(2):
-            for half in range(2):
+
+    group(0, 0)
+    pass_third(-1)
+    group(1, 0)
+    pass_third(1)
+    for copy in fq_copies:
+        copy.wait()
+    for n in range(8):
+        fq[:16, 64 * n : 64 * n + 64] = fq_got[n, :, :64]
+        fq[16:, 64 * n : 64 * n + 64] = fq_got[n, :, 64:]
+    fp[...] = jnp.zeros_like(fp)
+    pass_fourth(-1)
+    group(0, 3)
+    pass_fourth(1)
+    group(1, 3)
+    group(0, 1)
+    group(1, 1)
+
+    def query_step(n, carry):
+        queries_of(0, n)
+        queries_of(1, n)
+        return carry
+
+    lax.fori_loop(0, 2, query_step, 0)
+    lax.fori_loop(3, 4, query_step, 0)
+    for half in range(2):
+        for first in (0, -1, 1, 2):
+            for part in range(2):
                 arrived(half, first, 2, part)
-    groups(2, 3)
+        group(half, 2)
+    lax.fori_loop(2, 3, query_step, 0)
     fp_core = send(fp, got_fp, s_fp.at[0], r_fp.at[0], other)
     sum_copies = [
         send(sums, sums_all.at[n], s_sum.at[n], r_sum.at[n], peer) for n, peer in enumerate(tensor_peers)
@@ -582,7 +606,8 @@
 def shards(activations, gradients, proj_in, proj_out, damping, queries):
     act = activations.reshape(4, 4, 128, 1024)
     grad = gradients.reshape(4, 4, 128, 1024)
-    gram, back = main(act, grad, proj_in, proj_out, queries, damping.reshape(1, 128))
+    small = (proj_in, proj_out, queries, damping.reshape(1, 128))
+    gram, back = main(act, grad, *(pltpu.with_memory_space_constraint(value, pltpu.HBM) for value in small))
     gram, answer, residual = finish(gram, back)
     return answer, residual, gram
 

time: 108 us -> 104 us (0.963)
  local copies, waits for them, and re-layouts: 3.68 us -> 0 us
    unnamed x8 -> x0, local copies, waits for them, and re-layouts: 3.68 us -> none
where the time goes in v4:
time: 104 us
  Pallas kernels  103 us (99%)
    pallas_call x1, Pallas kernels, main(): pl.pallas_call(main_kernel, out_shape=(jax.ShapeDtypeStruct((2048, 8, 128...  98.8 us
    pallas_call x1, Pallas kernels, finish(): pl.pallas_call(finish_kernel, out_shape=(jax.ShapeDtypeStruct((2048, 8, 1...  4.17 us

profile of v4, /device:TPU:0, one launch (start us, length us, event | category | flops | bytes accessed | tf_op | source)
XLA Modules:
  0.0 103.7 jit_solution(14695306941386893504)
XLA Ops:
  0.6 98.8 %shard_map.85 = (f32[2048,8,128]{2,1,0:T(8,128)S(1)}, f32[16,2,32,128]{3,2,1,0:T(8,128)S(1)}) custom-call(f32[4,4,128,1024]{3,2,1,0:T(8,128)} %bitcast.3, f32[4,4,128,1024]{3,2,1,0:T(8,128)} %bitcast.4, f32[1024,128]{1,0:T(8,128)} %pin_hbm.1, f32[1024,128]{1,0:T(8,128)} %pout_hbm.1, f32[128,512]{1,0:T(8,128)} %q_hbm.1, f32[1,128]{1,0:T(1,128)} %bitcast.5), custom_call_target="tpu_custom_call" | custom-call | tf_op jit(solution)/shard_map/pallas_call | solution.py:485
  99.4 4.2 %shard_map.86 = (f32[2048,8,128]{2,1,0:T(8,128)}, f32[128,512]{1,0:T(8,128)}, f32[128,512]{1,0:T(8,128)}) custom-call(f32[2048,8,128]{2,1,0:T(8,128)S(1)} %get-tuple-element.8.gram, f32[16,2,32,128]{3,2,1,0:T(8,128)S(1)} %get-tuple-element.9.back), custom_call_target="tpu_custom_call" | custom-call | tf_op jit(solution)/shard_map/pallas_call | solution.py:592

commit v5 on v4

--- a/solution.py
+++ b/solution.py
@@ -276,20 +276,6 @@
             return p * 4 + shift(y, n, 4)
         return shift(x, n, 4) * 4 + p
 
-    for copy in query_copies:
-        copy.wait()
-    sums[...] = jnp.zeros_like(sums)
-    damps[...] = jnp.zeros_like(damps)
-    for at in range(16):
-        for half in range(2):
-            lane = 64 * ((at // 4 if half == 0 else at % 4) % 2)
-            damps[2 * at + half : 2 * at + half + 1, lane : lane + 64] = qr[at, 32:33, 64 * half : 64 * half + 64]
-    for half in range(2):
-        for n in range(4):
-            qg[half, n] = jnp.concatenate(
-                [qr[source(half, p, n), :, 64 * half : 64 * half + 64] for p in range(4)], axis=1
-            )
-
     for first in (-1, 1):
         for half in range(2):
             arrived(half, first, 0, None)
@@ -315,6 +301,20 @@
         zs[n].wait()
         from_d = shift(z, 4 - o, 4) * 2 + c
         cores.append(send(cols.at[from_d], cols.at[from_d], sx.at[n], rx.at[n], other))
+    for copy in query_copies:
+        copy.wait()
+    sums[...] = jnp.zeros_like(sums)
+    damps[...] = jnp.zeros_like(damps)
+    for at in range(16):
+        for half in range(2):
+            lane = 64 * ((at // 4 if half == 0 else at % 4) % 2)
+            damps[2 * at + half : 2 * at + half + 1, lane : lane + 64] = qr[at, 32:33, 64 * half : 64 * half + 64]
+    for half in range(2):
+        for n in range(4):
+            qg[half, n] = jnp.concatenate(
+                [qr[source(half, p, n), :, 64 * half : 64 * half + 64] for p in range(4)], axis=1
+            )
+
     for copy in cores:
         copy.wait()
 

time: 104 us -> 104 us (level)
  no operation moved by 1% of the time
where the time goes in v5:
time: 104 us
  Pallas kernels  103 us (99%)
    pallas_call x1, Pallas kernels, main(): pl.pallas_call(main_kernel, out_shape=(jax.ShapeDtypeStruct((2048, 8, 128...  98.8 us
    pallas_call x1, Pallas kernels, finish(): pl.pallas_call(finish_kernel, out_shape=(jax.ShapeDtypeStruct((2048, 8, 1...  4.17 us

profile of v5, /device:TPU:0, one launch (start us, length us, event | category | flops | bytes accessed | tf_op | source)
XLA Modules:
  0.0 103.7 jit_solution(17530095455302963505)
XLA Ops:
  0.6 98.8 %shard_map.85 = (f32[2048,8,128]{2,1,0:T(8,128)S(1)}, f32[16,2,32,128]{3,2,1,0:T(8,128)S(1)}) custom-call(f32[4,4,128,1024]{3,2,1,0:T(8,128)} %bitcast.3, f32[4,4,128,1024]{3,2,1,0:T(8,128)} %bitcast.4, f32[1024,128]{1,0:T(8,128)} %pin_hbm.1, f32[1024,128]{1,0:T(8,128)} %pout_hbm.1, f32[128,512]{1,0:T(8,128)} %q_hbm.1, f32[1,128]{1,0:T(1,128)} %bitcast.5), custom_call_target="tpu_custom_call" | custom-call | tf_op jit(solution)/shard_map/pallas_call | solution.py:485
  99.4 4.2 %shard_map.86 = (f32[2048,8,128]{2,1,0:T(8,128)}, f32[128,512]{1,0:T(8,128)}, f32[128,512]{1,0:T(8,128)}) custom-call(f32[2048,8,128]{2,1,0:T(8,128)S(1)} %get-tuple-element.8.gram, f32[16,2,32,128]{3,2,1,0:T(8,128)S(1)} %get-tuple-element.9.back), custom_call_target="tpu_custom_call" | custom-call | tf_op jit(solution)/shard_map/pallas_call | solution.py:592
